TPU v7x, 512 devices: a whole 4x8x8 slice. The times are simulated.
512 devices in a mesh: hst: 64 (over z, y), local: 8 (over x, core).
Axes of the slice: x: 4, y: 8, z: 8, core: 2. Of those that a mesh axis runs over, the one named last changes fastest.
Arguments:
- checkpoint: bfloat16 [64, 8, 64, 256], P(None, 'local', 'hst'), may hold values from -0.1875 to 0.1875
- counts: int32 [64, 4096, 512], P('hst', None, 'local'), may hold values from 0 to 2
- table_host: int32 [64], replicated, may hold values from 0 to 63, each once
- stored_slot: int32 [64], replicated, may hold values from 0 to 63, each once
- owner_order: int32 [4096], replicated, may hold values from 0 to 4095, each once
- fm_proj: bfloat16 [2, 64, 12], replicated, may hold values from -0.75 to 0.75
- fm_weight: bfloat16 [2, 768, 8192], P(None, None, 'local'), may hold values from -0.21875 to 0.21875
- fm_gain: float32 [2, 768], replicated, may hold values from 0.5 to 1.5
- lin_weight: bfloat16 [2, 32, 64], replicated, may hold values from -0.75 to 0.75
- out_gain: float32 [2, 256], replicated, may hold values from 0.5 to 1.5
Outputs:
- features: bfloat16 [4096, 64, 256], P(('hst', 'local'))
All inputs are finite; a program needn't handle non-finite values.
Results may differ from a plain program's by a relative error of at most 0.023.
Values may be sent and summed in bfloat16 or wider, within the bound.
No kernel may reach another device: no remote copies, remote signals or barrier semaphores. Data moves between devices by JAX's collectives and lax.ppermute only.
A program may use at most 64 MiB of HBM per device.

v0:
```python
import jax
import jax.numpy as jnp
from jax import lax
from jax.sharding import PartitionSpec as P

LAYERS = 2


def norm_rows(values, gain):
    mean = jnp.mean(values, axis=-1, keepdims=True)
    centered = values - mean
    spread = jnp.mean(centered * centered, axis=-1, keepdims=True)
    return centered * lax.rsqrt(spread + 1e-05) * gain


def wukong_layer(layer_state, projected_state, weight, gain, linear_output, out_scale):
    samples = layer_state.shape[0]
    inner_products = jnp.einsum(
        "pud,uj->pdj", layer_state, projected_state, preferred_element_type=jnp.float32
    ).astype(jnp.bfloat16)
    interaction_matrix = jnp.einsum(
        "ogx,oxl->ogl", layer_state, inner_products, preferred_element_type=jnp.float32
    )
    interaction_matrix = interaction_matrix.reshape(samples, -1)
    flat = norm_rows(interaction_matrix, gain).astype(jnp.bfloat16)
    column_part = jnp.dot(
        lax.all_gather(flat, "local", axis=0, tiled=True),
        weight,
        preferred_element_type=jnp.float32,
    ).astype(jnp.bfloat16)
    mixed = lax.all_to_all(column_part, "local", split_axis=0, concat_axis=1, tiled=True)
    mixed = mixed.reshape(samples, -1, layer_state.shape[2])
    compressed_state = jnp.einsum(
        "wp,jpo->jwo", linear_output, layer_state, preferred_element_type=jnp.float32
    )
    joined = jnp.concatenate(
        [mixed.astype(jnp.float32), compressed_state], axis=1
    ) + layer_state.astype(jnp.float32)
    return norm_rows(joined, out_scale).astype(jnp.bfloat16)


def shards(
    checkpoint,
    counts,
    table_host,
    stored_slot,
    owner_order,
    fm_proj,
    fm_weight,
    fm_gain,
    lin_weight,
    out_gain,
):
    host_count = lax.axis_size("hst")
    local_count = lax.axis_size("local")
    width = checkpoint.shape[-1]
    table_total = table_host.shape[0]
    samples = owner_order.shape[0] // (host_count * local_count)
    host_ids = jnp.arange(table_total, dtype=jnp.int32)
    source_slot = jnp.sum(
        jnp.where(table_host[None, :] == host_ids[:, None], stored_slot[None, :], 0), axis=1
    )
    outgoing = jnp.take(checkpoint, source_slot, axis=0)
    arrived = lax.all_to_all(outgoing, "hst", split_axis=0, concat_axis=2, tiled=True)
    table = arrived.reshape(-1, width)
    bag_rows = counts[0]
    bags = jnp.take(bag_rows, owner_order, axis=0).astype(jnp.bfloat16)
    partial_value = jnp.dot(bags, table, preferred_element_type=jnp.float32)
    partial_value = partial_value.reshape(host_count, local_count * samples, width)
    moved = lax.all_to_all(
        partial_value.astype(jnp.bfloat16), "hst", split_axis=0, concat_axis=0, tiled=True
    ).astype(partial_value.dtype)
    summed = lax.psum_scatter(moved.astype(jnp.bfloat16), "local", scatter_dimension=1, tiled=True)
    layer_state = jnp.transpose(jnp.take(summed, table_host, axis=0), (1, 0, 2))
    for layer in range(LAYERS):
        layer_state = wukong_layer(
            layer_state,
            fm_proj[layer],
            fm_weight[layer],
            fm_gain[layer],
            lin_weight[layer],
            out_gain[layer],
        )
    return layer_state


def solution(mesh):
    placed = (
        P(None, "local", "hst", None),
        P("hst", None, "local"),
        P(),
        P(),
        P(),
        P(),
        P(None, None, "local"),
        P(),
        P(),
        P(),
    )
    return jax.shard_map(
        shards,
        mesh=mesh,
        in_specs=placed,
        out_specs=P(("hst", "local"), None, None),
        check_vma=False,
    )
```

profile of v0, /device:TPU:1, one launch (start us, length us, event | category | flops | bytes accessed | tf_op | source)
XLA Modules:
  0.0 213.7 jit_solution(13688265621451760107)
XLA Ops:
  6.5 0.8 select_reduce_fusion
  7.4 0.7 gather_fusion.1
  8.1 0.1 bitcast_select_fusion
  8.2 0.5 broadcast.206
  8.7 0.7 reduce.8
  9.3 0.6 reshape.223
  10.0 17.1 %all-to-all-start = ((bf16[64,2,128]{2,1,0:T(2,128)(2,1)}), bf16[64,2,128]{2,1,0:T(2,128)(2,1)S(1)}, u32[]{:S(2)}, u32[]{:S(2)}) async-start(bf16[64,2,128]{2,1,0:T(2,128)(2,1)} %reshape.223), calls=%async_computation | async-start | bytes 65536 | tf_op jit(solution)/shard_map/all_to_all | solution.py:64
  27.2 0.7 fusion.27
  27.9 0.7 compare_and_fusion
  28.6 1.8 copy.57
  30.4 14.1 %gather_fusion = s32[4096,64]{1,0:T(8,128)} fusion(s32[4096,64]{1,0:T(8,128)S(1)} %bitcast.97, s32[4096]{0:T(1024)S(1)} %fusion.27), kind=kCustom, calls=%fused_computation | custom fusion | bytes 2113536 | tf_op jit(solution)/shard_map/jit(_take)/gather | solution.py:67
  44.5 3.6 %select_convert_fusion = bf16[4096,64]{1,0:T(8,128)(2,1)S(1)} fusion(s32[4096,64]{1,0:T(8,128)} %gather_fusion, pred[4096]{0:T(1024)(128)(4,1)S(1)} %compare_and_fusion), kind=kLoop, calls=%fused_computation.3 | loop fusion | flops 524288 | bytes 1576960 | tf_op jit(solution)/shard_map/convert_element_type | solution.py:67
  48.2 0.7 convolution_convert_fusion
  48.9 61.1 %all_to_all.40 = bf16[64,64,256]{2,1,0:T(8,128)(2,1)S(1)} all-to-all(bf16[64,64,256]{2,1,0:T(8,128)(2,1)S(1)} %convolution_convert_fusion), channel_id=1, replica_groups=mesh['hst'=64,'local'=8] {'hst'}, dimensions={0} | all-to-all | bytes 4194304 | tf_op jit(solution)/shard_map/all_to_all | solution.py:70
  110.0 1.5 copy.71
  111.5 0.6 copy-done.5
  112.3 37.1 %reduce-scatter.4.cloned.1.call-done = bf16[8,16384]{1,0:T(8,128)(2,1)} async-done(((bf16[64,16384]{1,0:T(8,128)(2,1)}), bf16[8,16384]{1,0:T(8,128)(2,1)}) %reduce-scatter.4.cloned.1.call-update) | async-done | bytes 262160
  149.4 1.0 copy.109
  150.4 0.2 copy.67
  150.6 0.6 gather_fusion.2
  151.2 0.5 fusion.35
  151.7 0.1 copy.61
  151.8 0.2 reshape.177
  152.0 0.2 multiply_reduce_fusion.3
  152.2 0.1 multiply_convert_fusion.3
  152.3 15.1 %all_gather.6 = bf16[64,768]{1,0:T(8,128)(2,1)S(1)} all-gather(bf16[8,768]{1,0:T(8,128)(2,1)S(1)} %multiply_convert_fusion.3), channel_id=1, replica_groups=mesh['hst'=64,'local'=8] {'local'}, dimensions={0}, use_global_device_ids=true | all-gather | bytes 110592 | tf_op jit(solution)/shard_map/all_gather | solution.py:27
  167.4 2.5 %fusion.15 = bf16[8,8,1024]{2,1,0:T(8,128)(2,1)} fusion(bf16[64,768]{1,0:T(8,128)(2,1)S(1)} %all_gather.6, bf16[2,768,1024]{2,1,0:T(8,128)(2,1)} %param.16), kind=kOutput, calls=%fused_computation.16 | convolution fusion | flops 100728832 | bytes 1802240 | tf_op jit(solution)/shard_map/dot_general | solution.py:26
  169.8 3.5 %all-to-all-start.2 = ((bf16[8,8,1024]{2,1,0:T(8,128)(2,1)}), bf16[8,8,1024]{2,1,0:T(8,128)(2,1)S(1)}, u32[]{:S(2)}, u32[]{:S(2)}) async-start(bf16[8,8,1024]{2,1,0:T(8,128)(2,1)} %fusion.15), calls=%async_computation.2 | async-start | bytes 262144 | tf_op jit(solution)/shard_map/all_to_all | solution.py:31
  173.3 0.2 convolution_bitcast_fusion.1
  173.5 5.0 %all-to-all-done.2 = bf16[8,8,1024]{2,1,0:T(8,128)(2,1)S(1)} async-done(((bf16[8,8,1024]{2,1,0:T(8,128)(2,1)}), bf16[8,8,1024]{2,1,0:T(8,128)(2,1)S(1)}, u32[]{:S(2)}, u32[]{:S(2)}) %all-to-all-start.2) | async-done | bytes 131104 | tf_op jit(solution)/shard_map/all_to_all | solution.py:31
  178.6 0.2 copy.62
  178.9 0.2 fusion.26
  179.1 0.3 multiply_reduce_fusion.1
  179.4 0.2 multiply_convert_fusion.1
  179.6 0.4 fusion.38
  180.0 0.1 copy.64
  180.2 0.2 reshape.178
  180.4 0.2 multiply_reduce_fusion.2
  180.6 0.1 multiply_convert_fusion.2
  180.7 13.4 %all_gather.7 = bf16[64,768]{1,0:T(8,128)(2,1)S(1)} all-gather(bf16[8,768]{1,0:T(8,128)(2,1)S(1)} %multiply_convert_fusion.2), channel_id=1, replica_groups=mesh['hst'=64,'local'=8] {'local'}, dimensions={0}, use_global_device_ids=true | all-gather | bytes 110592 | tf_op jit(solution)/shard_map/all_gather | solution.py:27
  194.1 2.5 %fusion.12 = bf16[8,8,1024]{2,1,0:T(8,128)(2,1)} fusion(bf16[64,768]{1,0:T(8,128)(2,1)S(1)} %all_gather.7, bf16[2,768,1024]{2,1,0:T(8,128)(2,1)} %param.16), kind=kOutput, calls=%fused_computation.15 | convolution fusion | flops 100728832 | bytes 1802240 | tf_op jit(solution)/shard_map/dot_general | solution.py:26
  196.5 3.5 %all-to-all-start.3 = ((bf16[8,8,1024]{2,1,0:T(8,128)(2,1)}), bf16[8,8,1024]{2,1,0:T(8,128)(2,1)S(1)}, u32[]{:S(2)}, u32[]{:S(2)}) async-start(bf16[8,8,1024]{2,1,0:T(8,128)(2,1)} %fusion.12), calls=%async_computation.3 | async-start | bytes 262144 | tf_op jit(solution)/shard_map/all_to_all | solution.py:31
  200.0 0.2 convolution_bitcast_fusion
  200.2 5.1 %all-to-all-done.3 = bf16[8,8,1024]{2,1,0:T(8,128)(2,1)S(1)} async-done(((bf16[8,8,1024]{2,1,0:T(8,128)(2,1)}), bf16[8,8,1024]{2,1,0:T(8,128)(2,1)S(1)}, u32[]{:S(2)}, u32[]{:S(2)}) %all-to-all-start.3) | async-done | bytes 131104 | tf_op jit(solution)/shard_map/all_to_all | solution.py:31
  205.3 0.2 copy.65
  205.5 0.1 fusion.25
  205.7 0.3 multiply_reduce_fusion
  206.0 0.9 multiply_convert_fusion
  (36 shorter events, 0.4 us)
Async XLA Ops:
  6.5 0.8 copy-start
  10.0 38.2 %all-to-all-start = ((bf16[64,2,128]{2,1,0:T(2,128)(2,1)}), bf16[64,2,128]{2,1,0:T(2,128)(2,1)S(1)}, u32[]{:S(2)}, u32[]{:S(2)}) async-start(bf16[64,2,128]{2,1,0:T(2,128)(2,1)} %reshape.223), calls=%async_computation | async-start | bytes 65536 | tf_op jit(solution)/shard_map/all_to_all | solution.py:64
  27.1 122.3 %reduce-scatter.4.cloned.1.call-start = ((), (), s32[]{:S(2)}) async-start(), calls=%async_computation.5 | async-start | bytes 2359296
  111.5 0.7 copy-start.5
  111.5 0.7 copy-start.3
  111.5 0.7 copy-start.4
  111.5 0.8 copy-start.1
  151.2 22.1 %copy-start.2 = (bf16[2,32,64]{2,1,0:T(8,128)(2,1)S(1)}, bf16[2,32,64]{2,1,0:T(8,128)(2,1)}, u32[]{:S(2)}) copy-start(bf16[2,32,64]{2,1,0:T(8,128)(2,1)} %param.18) | copy-start | bytes 24580
  169.8 8.7 %all-to-all-start.2 = ((bf16[8,8,1024]{2,1,0:T(8,128)(2,1)}), bf16[8,8,1024]{2,1,0:T(8,128)(2,1)S(1)}, u32[]{:S(2)}, u32[]{:S(2)}) async-start(bf16[8,8,1024]{2,1,0:T(8,128)(2,1)} %fusion.15), calls=%async_computation.2 | async-start | bytes 262144 | tf_op jit(solution)/shard_map/all_to_all | solution.py:31
  196.5 8.7 %all-to-all-start.3 = ((bf16[8,8,1024]{2,1,0:T(8,128)(2,1)}), bf16[8,8,1024]{2,1,0:T(8,128)(2,1)S(1)}, u32[]{:S(2)}, u32[]{:S(2)}) async-start(bf16[8,8,1024]{2,1,0:T(8,128)(2,1)} %fusion.12), calls=%async_computation.3 | async-start | bytes 262144 | tf_op jit(solution)/shard_map/all_to_all | solution.py:31
Sparse Core Ops, SparseCore 0:
  111.6 37.7 reduce-scatter.3
where the time goes:
time: 215 us; the launch traced here: 214 us
  blocking collectives  89.6 us (42%)
  waiting for transfers between devices  47.3 us (22%)
  starting transfers between devices  24.1 us (11%)
  local copies, waits for them, and re-layouts  22.8 us (11%)
  between operations  13.7 us (6%)
  other arithmetic  9.32 us (4%)
  matrix products  6.88 us (3%)
    all_to_all x1, blocking collectives, shards(): lax.all_to_all(partial_value.astype(jnp.bfloat16), 'hst', split_axis=0, c...  61.1 us
    unnamed x2, waiting for transfers between devices  37.1 us
    all_gather x2, blocking collectives, wukong_layer(): lax.all_gather(flat, 'local', axis=0, tiled=True)  28.5 us
    all_to_all x1, starting transfers between devices, shards(): lax.all_to_all(outgoing, 'hst', split_axis=0, concat_axis=2, tiled=True)  17.1 us
    gather x1, local copies, waits for them, and re-layouts, shards(): bags = jnp.take(bag_rows, owner_order, axis=0).astype(jnp.bfloat16)  14.1 us
    all_to_all x2, waiting for transfers between devices, wukong_layer(): lax.all_to_all(column_part, 'local', split_axis=0, concat_axis=1, tiled=T...  10.2 us
    all_to_all x2, starting transfers between devices, wukong_layer(): lax.all_to_all(column_part, 'local', split_axis=0, concat_axis=1, tiled=T...  6.91 us
    unnamed x18, local copies, waits for them, and re-layouts  5.78 us
  transfers between devices with their start and end apart: 4, of which 3 were waited for; matrix products, arithmetic and copies ran while one was open for 10% of the time, Pallas kernels for 0%

commit v1 on v0

--- a/solution.py
+++ b/solution.py
@@ -1,9 +1,79 @@
 import jax
 import jax.numpy as jnp
 from jax import lax
+from jax.experimental import pallas as pl
+from jax.experimental.pallas import tpu as pltpu
 from jax.sharding import PartitionSpec as P
 
 LAYERS = 2
+PACK = 4
+VMEM_LIMIT = 32 * 1024 * 1024
+
+
+def one_hot_rows(rows, positions):
+    number = lax.broadcasted_iota(jnp.int32, (rows, positions.shape[1]), 0)
+    return jnp.where(number == positions, 1.0, 0.0).astype(jnp.bfloat16)
+
+
+def pick_rows(host_ref, slot_ref, stored_ref, out_ref):
+    tables = stored_ref.shape[0]
+    holder = one_hot_rows(tables, host_ref[...])
+    slot = one_hot_rows(tables, slot_ref[...])
+    chosen = lax.dot_general(
+        holder, slot, (((1,), (1,)), ((), ())), preferred_element_type=jnp.float32
+    ).astype(jnp.bfloat16)
+    out_ref[:, 0, :] = jnp.dot(chosen, stored_ref[...], preferred_element_type=jnp.float32)
+
+
+def order_counts(counts_ref, order_ref, out_ref, packed_ref):
+    rows, samples = counts_ref.shape
+    words = rows // PACK
+    low_count = 256
+    high_count = samples // low_count
+    word = counts_ref[0:words, :]
+    for k in range(1, PACK):
+        word = word + (counts_ref[k * words : (k + 1) * words, :] << (2 * k))
+    word = word.astype(jnp.float32).astype(jnp.bfloat16)
+    for high in range(high_count):
+        packed_ref[high * words : (high + 1) * words, :] = word[
+            :, high * low_count : (high + 1) * low_count
+        ]
+    for target in range(order_ref.shape[0]):
+        number = order_ref[target : target + 1, :]
+        high_part = number >> 8
+        picked = jnp.dot(
+            packed_ref[...],
+            one_hot_rows(low_count, number & (low_count - 1)),
+            preferred_element_type=jnp.float32,
+        )
+        value = jnp.zeros((words, number.shape[1]), jnp.float32)
+        for high in range(high_count):
+            value = value + jnp.where(
+                high_part == high, picked[high * words : (high + 1) * words, :], 0.0
+            )
+        value = value.astype(jnp.int32)
+        for k in range(PACK):
+            out_ref[target, k * words : (k + 1) * words, :] = (
+                ((value >> (2 * k)) & 3).astype(jnp.float32).astype(jnp.bfloat16)
+            )
+
+
+def call(kernel, out_shape, *args, scratch=()):
+    return pl.pallas_call(
+        kernel,
+        out_shape=out_shape,
+        in_specs=[pl.BlockSpec(memory_space=pltpu.VMEM)] * len(args),
+        out_specs=pl.BlockSpec(memory_space=pltpu.VMEM),
+        scratch_shapes=list(scratch),
+        compiler_params=pltpu.CompilerParams(vmem_limit_bytes=VMEM_LIMIT),
+    )(*args)
+
+
+def gather_local(value):
+    count = lax.axis_size("local")
+    return lax.all_to_all(
+        jnp.broadcast_to(value[None], (count, *value.shape)), "local", 0, 0, tiled=False
+    )
 
 
 def norm_rows(values, gain):
@@ -23,11 +93,8 @@
     )
     interaction_matrix = interaction_matrix.reshape(samples, -1)
     flat = norm_rows(interaction_matrix, gain).astype(jnp.bfloat16)
-    column_part = jnp.dot(
-        lax.all_gather(flat, "local", axis=0, tiled=True),
-        weight,
-        preferred_element_type=jnp.float32,
-    ).astype(jnp.bfloat16)
+    gathered = gather_local(flat).reshape(-1, flat.shape[1])
+    column_part = jnp.dot(gathered, weight, preferred_element_type=jnp.float32).astype(jnp.bfloat16)
     mixed = lax.all_to_all(column_part, "local", split_axis=0, concat_axis=1, tiled=True)
     mixed = mixed.reshape(samples, -1, layer_state.shape[2])
     compressed_state = jnp.einsum(
@@ -51,27 +118,42 @@
     lin_weight,
     out_gain,
 ):
-    host_count = lax.axis_size("hst")
-    local_count = lax.axis_size("local")
+    hosts = lax.axis_size("hst")
+    locals_ = lax.axis_size("local")
     width = checkpoint.shape[-1]
-    table_total = table_host.shape[0]
-    samples = owner_order.shape[0] // (host_count * local_count)
-    host_ids = jnp.arange(table_total, dtype=jnp.int32)
-    source_slot = jnp.sum(
-        jnp.where(table_host[None, :] == host_ids[:, None], stored_slot[None, :], 0), axis=1
+    tables = table_host.shape[0]
+    batch = owner_order.shape[0]
+    samples = batch // (hosts * locals_)
+    rows = counts.shape[2]
+
+    order = jnp.transpose(owner_order.reshape(hosts, locals_, samples), (1, 0, 2))
+    ordered = call(
+        order_counts,
+        jax.ShapeDtypeStruct((locals_, rows, hosts * samples), jnp.bfloat16),
+        jnp.transpose(counts[0]),
+        order.reshape(locals_, hosts * samples),
+        scratch=[pltpu.VMEM((batch // 256 * (rows // PACK), 256), jnp.bfloat16)],
     )
-    outgoing = jnp.take(checkpoint, source_slot, axis=0)
-    arrived = lax.all_to_all(outgoing, "hst", split_axis=0, concat_axis=2, tiled=True)
-    table = arrived.reshape(-1, width)
-    bag_rows = counts[0]
-    bags = jnp.take(bag_rows, owner_order, axis=0).astype(jnp.bfloat16)
-    partial_value = jnp.dot(bags, table, preferred_element_type=jnp.float32)
-    partial_value = partial_value.reshape(host_count, local_count * samples, width)
-    moved = lax.all_to_all(
-        partial_value.astype(jnp.bfloat16), "hst", split_axis=0, concat_axis=0, tiled=True
-    ).astype(partial_value.dtype)
-    summed = lax.psum_scatter(moved.astype(jnp.bfloat16), "local", scatter_dimension=1, tiled=True)
-    layer_state = jnp.transpose(jnp.take(summed, table_host, axis=0), (1, 0, 2))
+    bags = lax.all_to_all(ordered, "local", 0, 0, tiled=False)
+
+    outgoing = call(
+        pick_rows,
+        jax.ShapeDtypeStruct((tables, 1, width), jnp.float32),
+        table_host.reshape(1, tables),
+        stored_slot.reshape(1, tables),
+        checkpoint.reshape(tables, width),
+    )
+    arrived = lax.all_to_all(outgoing, "hst", 0, 0, tiled=False)
+    table = gather_local(arrived.reshape(tables, width).astype(jnp.bfloat16))
+
+    pooled = lax.dot_general(
+        bags.reshape(-1, hosts * samples),
+        table.reshape(-1, width),
+        (((0,), (0,)), ((), ())),
+        preferred_element_type=jnp.float32,
+    ).astype(jnp.bfloat16)
+    moved = lax.all_to_all(pooled.reshape(hosts, samples, width), "hst", 0, 0, tiled=False)
+    layer_state = jnp.transpose(jnp.take(moved, table_host, axis=0), (1, 0, 2))
     for layer in range(LAYERS):
         layer_state = wukong_layer(
             layer_state,

time: 215 us -> 128 us (0.60)
  blocking collectives: 89.6 us -> 36 us
  local copies, waits for them, and re-layouts: 22.8 us -> 6.93 us
  between operations: 13.7 us -> 0.3 us
  waiting for transfers between devices: 47.3 us -> 40.8 us
  starting transfers between devices: 24.1 us -> 30.3 us
  other arithmetic: 9.32 us -> 3.6 us
  Pallas kernels: 0 us -> 2.18 us
    unnamed x2 -> x0, waiting for transfers between devices: 37.1 us -> none
    all_to_all x1 -> x4, waiting for transfers between devices: 0.01 us -> 30.7 us  [the longest x1 12.7 us: shards(): lax.all_to_all(pooled.reshape(hosts, samples, width), 'hst', 0, 0, tiled=...]
    all_gather x2 -> x0, blocking collectives: 28.5 us -> none  [wukong_layer(): lax.all_gather(flat, 'local', axis=0, tiled=True)]
    all_to_all x1 -> x2, blocking collectives: 61.1 us -> 36 us  [the longest x1 27.8 us: shards(): arrived = lax.all_to_all(outgoing, 'hst', 0, 0, tiled=False)]
    gather x3 -> x1, local copies, waits for them, and re-layouts: 15.4 us -> 0.59 us  [shards(): layer_state = jnp.transpose(jnp.take(moved, table_host, axis=0), (1, 0, 2))]
    all_to_all x1 -> x4, starting transfers between devices: 17.1 us -> 22.1 us  [the longest x2 12.9 us: gather_local(): lax.all_to_all(jnp.broadcast_to(value[None], (count, *value.shape)), 'loc...]
    convert_element_type x1 -> x0, other arithmetic: 3.61 us -> none  [shards(): bags = jnp.take(bag_rows, owner_order, axis=0).astype(jnp.bfloat16)]
    unnamed x18 -> x22, local copies, waits for them, and re-layouts: 5.78 us -> 2.73 us
  transfers between devices with their start and end apart: 4 -> 6, of which waited for: 3 -> 6; matrix products, arithmetic and copies ran while one was open for 10% -> 1% of each run, Pallas kernels for 0% -> 1%
where the time goes in v1:
time: 128 us; the launch traced here: 127 us
  waiting for transfers between devices  40.8 us (32%)
  blocking collectives  36 us (28%)
  starting transfers between devices  30.3 us (24%)
  matrix products  7.27 us (6%)
  local copies, waits for them, and re-layouts  6.93 us (5%)
  other arithmetic  3.6 us (3%)
  Pallas kernels  2.18 us (2%)
    all_to_all x1, blocking collectives, shards(): arrived = lax.all_to_all(outgoing, 'hst', 0, 0, tiled=False)  27.8 us
    all_to_all x2, starting transfers between devices, gather_local(): lax.all_to_all(jnp.broadcast_to(value[None], (count, *value.shape)), 'loc...  12.9 us
    all_to_all x1, waiting for transfers between devices, shards(): lax.all_to_all(pooled.reshape(hosts, samples, width), 'hst', 0, 0, tiled=...  12.7 us
    all_to_all x2, waiting for transfers between devices, wukong_layer(): lax.all_to_all(column_part, 'local', split_axis=0, concat_axis=1, tiled=T...  10.2 us
    all_to_all x1, waiting for transfers between devices, shards(): bags = lax.all_to_all(ordered, 'local', 0, 0, tiled=False)  9.45 us
    all_to_all x2, waiting for transfers between devices, gather_local(): lax.all_to_all(jnp.broadcast_to(value[None], (count, *value.shape)), 'loc...  8.48 us
    all_to_all x1, blocking collectives, gather_local(): lax.all_to_all(jnp.broadcast_to(value[None], (count, *value.shape)), 'loc...  8.22 us
    all_to_all x2, starting transfers between devices, wukong_layer(): lax.all_to_all(column_part, 'local', split_axis=0, concat_axis=1, tiled=T...  8.19 us
  transfers between devices with their start and end apart: 6, of which 6 were waited for; matrix products, arithmetic and copies ran while one was open for 1% of the time, Pallas kernels for 1%

profile of v1, /device:TPU:1, one launch (start us, length us, event | category | flops | bytes accessed | tf_op | source)
XLA Modules:
  0.0 127.4 jit_solution(1916087065378510183)
XLA Ops:
  0.0 0.8 copy-done.1
  0.9 0.7 copy-done.2
  1.5 0.7 copy-done.3
  2.2 0.3 shard_map.101
  2.5 0.5 broadcast.170
  3.0 0.8 reduce.8
  3.9 27.8 %all_to_all.56 = bf16[64,2,128]{2,1,0:T(2,128)(2,1)S(1)} all-to-all(bf16[64,2,128]{2,1,0:T(2,128)(2,1)S(1)} %reshape.242), channel_id=1, replica_groups=mesh['hst'=64,'local'=8] {'hst'}, dimensions={0} | all-to-all | bytes 65536 | tf_op jit(solution)/shard_map/all_to_all | solution.py:146
  31.7 0.7 broadcast_in_dim.19
  32.4 6.5 %all-to-all-start.2 = ((bf16[8,64,256]{2,1,0:T(8,128)(2,1)}), bf16[8,64,256]{2,1,0:T(8,128)(2,1)S(1)}, u32[]{:S(2)}, u32[]{:S(2)}) async-start(bf16[8,64,256]{2,1,0:T(8,128)(2,1)} %broadcast_in_dim.19), calls=%async_computation.2 | async-start | bytes 524288 | tf_op jit(solution)/shard_map/all_to_all | solution.py:74
  38.9 0.9 reshape.214
  39.9 0.2 reshape.215.order_ref
  40.0 1.9 %shard_map.100 = bf16[8,64,512]{2,1,0:T(8,128)(2,1)} custom-call(s32[64,4096]{1,0:T(8,128)S(1)} %bitcast.96, s32[8,512]{1,0:T(8,128)S(1)} %reshape.215.order_ref), custom_call_target="tpu_custom_call" | custom-call | tf_op jit(solution)/shard_map/pallas_call | solution.py:62
  41.9 3.5 %all-to-all-done.2 = bf16[8,64,256]{2,1,0:T(8,128)(2,1)S(1)} async-done(((bf16[8,64,256]{2,1,0:T(8,128)(2,1)}), bf16[8,64,256]{2,1,0:T(8,128)(2,1)S(1)}, u32[]{:S(2)}, u32[]{:S(2)}) %all-to-all-start.2) | async-done | bytes 262176 | tf_op jit(solution)/shard_map/all_to_all | solution.py:74
  45.4 4.4 %all-to-all-start = ((bf16[8,64,512]{2,1,0:T(8,128)(2,1)}), bf16[8,64,512]{2,1,0:T(8,128)(2,1)S(1)}, u32[]{:S(2)}, u32[]{:S(2)}) async-start(bf16[8,64,512]{2,1,0:T(8,128)(2,1)} %shard_map.100), calls=%async_computation | async-start | bytes 1048576 | tf_op jit(solution)/shard_map/all_to_all | solution.py:137
  49.9 9.4 %all-to-all-done = bf16[8,64,512]{2,1,0:T(8,128)(2,1)S(1)} async-done(((bf16[8,64,512]{2,1,0:T(8,128)(2,1)}), bf16[8,64,512]{2,1,0:T(8,128)(2,1)S(1)}, u32[]{:S(2)}, u32[]{:S(2)}) %all-to-all-start) | async-done | bytes 524320 | tf_op jit(solution)/shard_map/all_to_all | solution.py:137
  59.4 1.1 fusion.7
  60.4 4.8 %all-to-all-start.3 = ((bf16[64,8,256]{2,1,0:T(8,128)(2,1)}), bf16[64,8,256]{2,1,0:T(8,128)(2,1)S(1)}, u32[]{:S(2)}, u32[]{:S(2)}) async-start(bf16[64,8,256]{2,1,0:T(8,128)(2,1)} %fusion.7), calls=%async_computation.3 | async-start | bytes 524288 | tf_op jit(solution)/shard_map/all_to_all | solution.py:155
  65.2 12.7 %all-to-all-done.3 = bf16[64,8,256]{2,1,0:T(8,128)(2,1)S(1)} async-done(((bf16[64,8,256]{2,1,0:T(8,128)(2,1)}), bf16[64,8,256]{2,1,0:T(8,128)(2,1)S(1)}, u32[]{:S(2)}, u32[]{:S(2)}) %all-to-all-start.3) | async-done | bytes 262176 | tf_op jit(solution)/shard_map/all_to_all | solution.py:155
  78.0 0.6 gather_fusion
  78.6 0.5 fusion.35
  79.1 0.1 copy.24
  79.2 0.2 reshape.220
  79.4 0.2 multiply_reduce_fusion.3
  79.7 0.7 broadcast_in_dim.22
  80.4 6.4 %all-to-all-start.4 = ((bf16[8,8,768]{2,1,0:T(8,128)(2,1)}), bf16[8,8,768]{2,1,0:T(8,128)(2,1)S(1)}, u32[]{:S(2)}, u32[]{:S(2)}) async-start(bf16[8,8,768]{2,1,0:T(8,128)(2,1)} %broadcast_in_dim.22), calls=%async_computation.4 | async-start | bytes 196608 | tf_op jit(solution)/shard_map/all_to_all | solution.py:74
  86.7 5.0 %all-to-all-done.4 = bf16[8,8,768]{2,1,0:T(8,128)(2,1)S(1)} async-done(((bf16[8,8,768]{2,1,0:T(8,128)(2,1)}), bf16[8,8,768]{2,1,0:T(8,128)(2,1)S(1)}, u32[]{:S(2)}, u32[]{:S(2)}) %all-to-all-start.4) | async-done | bytes 98336 | tf_op jit(solution)/shard_map/all_to_all | solution.py:74
  91.7 2.5 %fusion.17 = bf16[8,8,1024]{2,1,0:T(8,128)(2,1)} fusion(bf16[2,768,1024]{2,1,0:T(8,128)(2,1)} %param.16, bf16[8,8,768]{2,1,0:T(8,128)(2,1)S(1)} %all-to-all-done.4), kind=kOutput, calls=%fused_computation.15 | convolution fusion | flops 100728832 | bytes 1802240 | tf_op jit(solution)/shard_map/dot_general | solution.py:97
  94.2 4.1 %all-to-all-start.5 = ((bf16[8,8,1024]{2,1,0:T(8,128)(2,1)}), bf16[8,8,1024]{2,1,0:T(8,128)(2,1)S(1)}, u32[]{:S(2)}, u32[]{:S(2)}) async-start(bf16[8,8,1024]{2,1,0:T(8,128)(2,1)} %fusion.17), calls=%async_computation.5 | async-start | bytes 262144 | tf_op jit(solution)/shard_map/all_to_all | solution.py:98
  98.3 0.2 convolution_bitcast_fusion.2
  98.5 5.0 %all-to-all-done.5 = bf16[8,8,1024]{2,1,0:T(8,128)(2,1)S(1)} async-done(((bf16[8,8,1024]{2,1,0:T(8,128)(2,1)}), bf16[8,8,1024]{2,1,0:T(8,128)(2,1)S(1)}, u32[]{:S(2)}, u32[]{:S(2)}) %all-to-all-start.5) | async-done | bytes 131104 | tf_op jit(solution)/shard_map/all_to_all | solution.py:98
  103.6 0.2 copy.25
  103.8 0.2 fusion.28
  104.1 0.3 multiply_reduce_fusion.1
  104.4 0.2 multiply_convert_fusion.1
  104.6 0.4 fusion.38
  105.0 0.1 copy.27
  105.2 0.2 reshape.222
  105.4 0.2 multiply_reduce_fusion.2
  105.6 0.1 multiply_convert_fusion.2
  105.7 8.2 %all_to_all.57 = bf16[8,8,768]{2,1,0:T(8,128)(2,1)S(1)} all-to-all(bf16[8,8,768]{2,1,0:T(8,128)(2,1)S(1)} %broadcast_in_dim.23), channel_id=1, replica_groups=mesh['hst'=64,'local'=8] {'local'}, dimensions={0} | all-to-all | bytes 196608 | tf_op jit(solution)/shard_map/all_to_all | solution.py:74
  113.9 2.5 %fusion.14 = bf16[8,8,1024]{2,1,0:T(8,128)(2,1)} fusion(bf16[2,768,1024]{2,1,0:T(8,128)(2,1)} %param.16, bf16[8,8,768]{2,1,0:T(8,128)(2,1)S(1)} %all_to_all.57), kind=kOutput, calls=%fused_computation.14 | convolution fusion | flops 100728832 | bytes 1802240 | tf_op jit(solution)/shard_map/dot_general | solution.py:97
  116.4 4.1 %all-to-all-start.7 = ((bf16[8,8,1024]{2,1,0:T(8,128)(2,1)}), bf16[8,8,1024]{2,1,0:T(8,128)(2,1)S(1)}, u32[]{:S(2)}, u32[]{:S(2)}) async-start(bf16[8,8,1024]{2,1,0:T(8,128)(2,1)} %fusion.14), calls=%async_computation.7 | async-start | bytes 262144 | tf_op jit(solution)/shard_map/all_to_all | solution.py:98
  120.5 0.2 convolution_bitcast_fusion.1
  120.6 5.1 %all-to-all-done.7 = bf16[8,8,1024]{2,1,0:T(8,128)(2,1)S(1)} async-done(((bf16[8,8,1024]{2,1,0:T(8,128)(2,1)}), bf16[8,8,1024]{2,1,0:T(8,128)(2,1)S(1)}, u32[]{:S(2)}, u32[]{:S(2)}) %all-to-all-start.7) | async-done | bytes 131104 | tf_op jit(solution)/shard_map/all_to_all | solution.py:98
  125.8 0.2 copy.28
  126.0 0.2 fusion.27
  126.2 0.3 multiply_reduce_fusion
  126.5 0.9 multiply_convert_fusion
  (40 shorter events, 0.5 us)
Async XLA Ops:
  0.0 40.0 %copy-start = (s32[1,4096,64]{1,2,0:T(8,128)S(1)}, s32[1,4096,64]{1,2,0:T(8,128)}, u32[]{:S(2)}) copy-start(s32[1,4096,64]{1,2,0:T(8,128)} %param.11) | copy-start | bytes 3145732
  0.0 0.8 copy-start.1
  0.8 0.7 copy-start.2
  1.5 0.7 copy-start.3
  2.2 47.7 %copy-start.7 = (f32[2,768]{1,0:T(2,128)S(1)}, f32[2,768]{1,0:T(2,128)}, u32[]{:S(2)}) copy-start(f32[2,768]{1,0:T(2,128)} %param.17) | copy-start | bytes 18436
  2.2 47.7 %copy-start.4 = (s32[64]{0:T(128)S(1)}, s32[64]{0:T(128)}, u32[]{:S(2)}) copy-start(s32[64]{0:T(128)} %param.12) | copy-start | bytes 772
  32.4 32.8 %copy-start.5 = (bf16[2,64,12]{1,0,2:T(2,128)(2,1)S(1)}, bf16[2,64,12]{1,0,2:T(2,128)(2,1)}, u32[]{:S(2)}) copy-start(bf16[2,64,12]{1,0,2:T(2,128)(2,1)} %param.15) | copy-start | bytes 9220
  32.4 13.0 %all-to-all-start.2 = ((bf16[8,64,256]{2,1,0:T(8,128)(2,1)}), bf16[8,64,256]{2,1,0:T(8,128)(2,1)S(1)}, u32[]{:S(2)}, u32[]{:S(2)}) async-start(bf16[8,64,256]{2,1,0:T(8,128)(2,1)} %broadcast_in_dim.19), calls=%async_computation.2 | async-start | bytes 524288 | tf_op jit(solution)/shard_map/all_to_all | solution.py:74
  41.9 44.8 %copy-start.8 = (f32[2,256]{1,0:T(2,128)S(1)}, f32[2,256]{1,0:T(2,128)}, u32[]{:S(2)}) copy-start(f32[2,256]{1,0:T(2,128)} %param.19) | copy-start | bytes 6148
  45.4 13.9 %all-to-all-start = ((bf16[8,64,512]{2,1,0:T(8,128)(2,1)}), bf16[8,64,512]{2,1,0:T(8,128)(2,1)S(1)}, u32[]{:S(2)}, u32[]{:S(2)}) async-start(bf16[8,64,512]{2,1,0:T(8,128)(2,1)} %shard_map.100), calls=%async_computation | async-start | bytes 1048576 | tf_op jit(solution)/shard_map/all_to_all | solution.py:137
  60.4 37.9 %copy-start.6 = (bf16[2,32,64]{2,1,0:T(8,128)(2,1)S(1)}, bf16[2,32,64]{2,1,0:T(8,128)(2,1)}, u32[]{:S(2)}) copy-start(bf16[2,32,64]{2,1,0:T(8,128)(2,1)} %param.18) | copy-start | bytes 24580
  60.4 17.6 %all-to-all-start.3 = ((bf16[64,8,256]{2,1,0:T(8,128)(2,1)}), bf16[64,8,256]{2,1,0:T(8,128)(2,1)S(1)}, u32[]{:S(2)}, u32[]{:S(2)}) async-start(bf16[64,8,256]{2,1,0:T(8,128)(2,1)} %fusion.7), calls=%async_computation.3 | async-start | bytes 524288 | tf_op jit(solution)/shard_map/all_to_all | solution.py:155
  80.4 11.4 %all-to-all-start.4 = ((bf16[8,8,768]{2,1,0:T(8,128)(2,1)}), bf16[8,8,768]{2,1,0:T(8,128)(2,1)S(1)}, u32[]{:S(2)}, u32[]{:S(2)}) async-start(bf16[8,8,768]{2,1,0:T(8,128)(2,1)} %broadcast_in_dim.22), calls=%async_computation.4 | async-start | bytes 196608 | tf_op jit(solution)/shard_map/all_to_all | solution.py:74
  94.2 9.4 %all-to-all-start.5 = ((bf16[8,8,1024]{2,1,0:T(8,128)(2,1)}), bf16[8,8,1024]{2,1,0:T(8,128)(2,1)S(1)}, u32[]{:S(2)}, u32[]{:S(2)}) async-start(bf16[8,8,1024]{2,1,0:T(8,128)(2,1)} %fusion.17), calls=%async_computation.5 | async-start | bytes 262144 | tf_op jit(solution)/shard_map/all_to_all | solution.py:98
  116.4 9.4 %all-to-all-start.7 = ((bf16[8,8,1024]{2,1,0:T(8,128)(2,1)}), bf16[8,8,1024]{2,1,0:T(8,128)(2,1)S(1)}, u32[]{:S(2)}, u32[]{:S(2)}) async-start(bf16[8,8,1024]{2,1,0:T(8,128)(2,1)} %fusion.14), calls=%async_computation.7 | async-start | bytes 262144 | tf_op jit(solution)/shard_map/all_to_all | solution.py:98

commit v2 on v0

v2 whole, which is shorter than its diff:
```python
import jax
import jax.numpy as jnp
from jax import lax
from jax.experimental import pallas as pl
from jax.experimental.pallas import tpu as pltpu
from jax.sharding import PartitionSpec as P

LAYERS = 2
PACK = 4
LOW = 256
LANES = 128
VMEM_LIMIT = 40 * 1024 * 1024
F32 = jnp.float32
BF16 = jnp.bfloat16


def number(shape, axis):
    return lax.broadcasted_iota(jnp.int32, shape, axis)


def ones_where(condition):
    return jnp.where(condition, 1.0, 0.0).astype(BF16)


def matmul(a, b):
    return jnp.dot(a, b, preferred_element_type=F32)


def matmul_nt(a, b):
    return lax.dot_general(a, b, (((1,), (1,)), ((), ())), preferred_element_type=F32)


def matmul_tn(a, b):
    return lax.dot_general(a, b, (((0,), (0,)), ((), ())), preferred_element_type=F32)


def pick_rows(host_ref, slot_ref, stored_ref, out_ref):
    tables = stored_ref.shape[0]
    holder = ones_where(number((tables, tables), 0) == host_ref[...])
    slot = ones_where(number((tables, tables), 0) == slot_ref[...])
    chosen = matmul_nt(holder, slot).astype(BF16)
    out_ref[:, 0, :] = matmul(chosen, stored_ref[...])


def order_counts(after_ref, counts_ref, order_ref, out_ref, packed_ref):
    rows, batch = counts_ref.shape
    targets, _, length = out_ref.shape
    words = rows // PACK
    high_count = batch // LOW
    order_rows = order_ref.shape[0]
    samples = 8
    word = counts_ref[0:words, :]
    for k in range(1, PACK):
        word = word + (counts_ref[k * words : (k + 1) * words, :] << (2 * k))
    word = word.astype(F32).astype(BF16)
    for high in range(high_count):
        packed_ref[high * words : (high + 1) * words, :] = word[:, high * LOW : (high + 1) * LOW]
    order = order_ref[...]
    parts = jnp.concatenate([order >> 8, order & (LOW - 1)], axis=0).astype(F32).astype(BF16)
    for target in range(targets):
        m = number((LANES, length), 1)
        row = (m // samples) * (targets * samples) + target * samples + m % samples
        found = matmul(parts, ones_where(number((LANES, length), 0) == row % LANES))
        m = number((2 * order_rows, length), 1)
        row = (m // samples) * (targets * samples) + target * samples + m % samples
        found = jnp.where(
            number((2 * order_rows, length), 0) % order_rows == row // LANES, found, 0.0
        )
        high_part = jnp.sum(found[:order_rows], axis=0, keepdims=True).astype(jnp.int32)
        low_part = jnp.sum(found[order_rows:], axis=0, keepdims=True).astype(jnp.int32)
        picked = matmul(packed_ref[...], ones_where(number((LOW, length), 0) == low_part))
        value = jnp.zeros((words, length), F32)
        for high in range(high_count):
            value = value + jnp.where(
                high_part == high, picked[high * words : (high + 1) * words, :], 0.0
            )
        value = value.astype(jnp.int32)
        for k in range(PACK):
            out_ref[target, k * words : (k + 1) * words, :] = (
                ((value >> (2 * k)) & 3).astype(F32).astype(BF16)
            )


def join_table(arrived_ref, ordered_ref, out_ref):
    length = ordered_ref.shape[2]
    table = arrived_ref[:, 0, :].astype(BF16)
    for target in range(out_ref.shape[0]):
        out_ref[target, :, :length] = ordered_ref[target]
        out_ref[target, :, length:] = table


def pool(both_ref, out_ref):
    length = out_ref.shape[0]
    out_ref[...] = matmul_tn(both_ref[:, :length], both_ref[:, length:]).astype(BF16)


def spread(rows, columns, samples, of_rows):
    if of_rows:
        return ones_where(number((rows, columns), 0) // samples == number((rows, columns), 1))
    return ones_where(number((rows, columns), 1) // samples == number((rows, columns), 0))


def same_sample(rows, columns, samples):
    return number((rows, columns), 0) % samples == number((rows, columns), 1) % samples


def prepare(
    after_ref, host_ref, proj_ref, lin_ref, weight_ref, gain_ref,
    place_ref, proj_out_ref, lin_out_ref, weight_out_ref, gain_out_ref,
):
    layers, rank, tables = proj_ref.shape
    state = place_ref.shape[0]
    samples = state // tables
    flat = gain_ref.shape[1]
    ranks = flat // tables
    wide = spread(tables, state, samples, False)
    holder = ones_where(number((tables, tables), 0) == host_ref[...])
    chosen = matmul_nt(spread(state, tables, samples, True), holder).astype(BF16)
    place = matmul(chosen, wide)
    place_ref[...] = jnp.where(same_sample(state, state, samples), place, 0.0).astype(BF16)
    row = number((flat, flat), 0)
    turn = ones_where((row % tables) * ranks + row // tables == number((flat, flat), 1))
    column = number((flat, flat), 1)
    turn_back = ones_where((column % tables) * ranks + column // tables == number((flat, flat), 0))
    gain = gain_ref[...]
    total = jnp.zeros(gain.shape, F32)
    for _ in range(3):
        part = gain.astype(BF16)
        total = total + matmul(part, turn_back)
        gain = gain - part.astype(F32)
    gain_out_ref[...] = total
    for layer in range(layers):
        tall = spread(proj_out_ref.shape[1], rank, samples, True)
        values = matmul(matmul(tall, proj_ref[layer]).astype(BF16), wide)
        keep = same_sample(proj_out_ref.shape[1], state, samples)
        proj_out_ref[layer] = jnp.where(keep, values, 0.0).astype(BF16)
        tall = spread(lin_out_ref.shape[1], lin_ref.shape[1], samples, True)
        values = matmul(matmul(tall, lin_ref[layer]).astype(BF16), wide)
        keep = same_sample(lin_out_ref.shape[1], state, samples)
        lin_out_ref[layer] = jnp.where(keep, values, 0.0).astype(BF16)
        for start in range(0, weight_ref.shape[2], 256):
            weight_out_ref[layer, :, start : start + 256] = matmul(
                turn, weight_ref[layer, :, start : start + 256]
            ).astype(BF16)


def norm_rows(values, gain):
    mean = jnp.mean(values, axis=-1, keepdims=True)
    centered = values - mean
    spread_ = jnp.mean(centered * centered, axis=-1, keepdims=True)
    return centered * lax.rsqrt(spread_ + 1e-05) * gain


def by_sample(state):
    rows = state.shape[0]
    samples = 8
    row = number((rows, rows), 0)
    tables = rows // samples
    turn = ones_where((row % tables) * samples + row // tables == number((rows, rows), 1))
    return matmul(turn, state).astype(BF16)


def interactions(state, turned, proj, gain, flat_ref):
    rows = state.shape[0]
    samples = flat_ref.shape[1]
    tables = rows // samples
    inner = matmul(proj, state).astype(BF16)
    inter = matmul_nt(inner, turned)
    own = number(inter.shape, 0) % samples == number(inter.shape, 1) // tables
    inter = jnp.where(own, inter, 0.0)
    while inter.shape[1] > LANES:
        half = inter.shape[1] // 2
        inter = inter[:, :half] + inter[:, half:]
    inter = inter + pltpu.roll(inter, tables, 1)
    first = number((samples, LANES), 1) < tables
    flat = jnp.concatenate(
        [
            jnp.where(first, inter[at : at + samples], inter[at + samples : at + 2 * samples])
            for at in range(0, inter.shape[0], 2 * samples)
        ],
        axis=1,
    )
    flat = norm_rows(flat, gain).astype(BF16)
    for target in range(flat_ref.shape[0]):
        flat_ref[target] = flat


def first_layer(moved_ref, place_ref, proj_ref, gain_ref, state_ref, flat_ref):
    state = matmul(place_ref[...], moved_ref[...]).astype(BF16)
    state_ref[...] = state
    interactions(state, by_sample(state), proj_ref[0], gain_ref[0:1, :], flat_ref)


def map_columns(layer, flat_ref, weight_ref, out_ref):
    out_ref[...] = matmul(flat_ref[...], weight_ref[layer]).astype(BF16)


def next_state(mixed_ref, state, lin, scale):
    width = state.shape[1]
    compressed = matmul(lin, state)
    mixed = [
        mixed_ref[source, :, start : start + width].astype(F32)
        for source in range(mixed_ref.shape[0])
        for start in range(0, mixed_ref.shape[2], width)
    ]
    joined = jnp.concatenate([*mixed, compressed], axis=0) + state.astype(F32)
    return norm_rows(joined, scale).astype(BF16)


def next_layer(layer, mixed_ref, old_ref, lin_ref, scale_ref, proj_ref, gain_ref, state_ref, flat_ref):
    state = next_state(mixed_ref, old_ref[...], lin_ref[layer], scale_ref[layer : layer + 1, :])
    state_ref[...] = state
    interactions(
        state, by_sample(state), proj_ref[layer + 1], gain_ref[layer + 1 : layer + 2, :], flat_ref
    )


def last_state(layer, mixed_ref, old_ref, lin_ref, scale_ref, out_ref):
    out_ref[...] = by_sample(
        next_state(mixed_ref, old_ref[...], lin_ref[layer], scale_ref[layer : layer + 1, :])
    )


def call(kernel, out_shape, *args, after=(), scratch=(), flops=0):
    moved = sum(a.size * a.dtype.itemsize for a in args)
    return pl.pallas_call(
        kernel,
        out_shape=out_shape,
        in_specs=[pl.BlockSpec(memory_space=pl.ANY)] * len(after)
        + [pl.BlockSpec(memory_space=pltpu.VMEM)] * len(args),
        out_specs=jax.tree.map(lambda _: pl.BlockSpec(memory_space=pltpu.VMEM), out_shape),
        scratch_shapes=list(scratch),
        compiler_params=pltpu.CompilerParams(vmem_limit_bytes=VMEM_LIMIT),
        cost_estimate=pl.CostEstimate(flops=flops, bytes_accessed=moved, transcendentals=0),
    )(*after, *args)


def exchange(value, axis):
    return lax.all_to_all(value, axis, 0, 0, tiled=False)


def shards(
    checkpoint,
    counts,
    table_host,
    stored_slot,
    owner_order,
    fm_proj,
    fm_weight,
    fm_gain,
    lin_weight,
    out_gain,
):
    hosts = lax.axis_size("hst")
    locals_ = lax.axis_size("local")
    width = checkpoint.shape[-1]
    tables = table_host.shape[0]
    batch = owner_order.shape[0]
    samples = batch // (hosts * locals_)
    rows = counts.shape[2]
    length = hosts * samples
    state_rows = tables * samples
    rank = fm_proj.shape[2]
    flat_size = tables * rank
    lin_rows = lin_weight.shape[1] * samples

    def shape(dims, dtype=BF16):
        return jax.ShapeDtypeStruct(dims, dtype)

    outgoing = call(
        pick_rows,
        shape((tables, 1, width), F32),
        table_host.reshape(1, tables),
        stored_slot.reshape(1, tables),
        checkpoint.reshape(tables, width),
    )
    arrived = exchange(outgoing, "hst")
    ordered = call(
        order_counts,
        shape((locals_, rows, length)),
        jnp.transpose(counts[0]),
        owner_order.reshape(batch // LANES, LANES),
        after=(outgoing,),
        scratch=[pltpu.VMEM((batch // LOW * (rows // PACK), LOW), BF16)],
        flops=2 * batch * (LOW * LOW + 64 * LANES),
    )
    both = exchange(
        call(join_table, shape((locals_, rows, length + width)), arrived, ordered), "local"
    )
    pooled = call(pool, shape((length, width)), both.reshape(locals_ * rows, length + width))
    moved = exchange(pooled.reshape(hosts, samples, width), "hst")

    proj_rows = -(-rank // 16) * 16
    place, proj, lin, weight, gain = call(
        prepare,
        (
            shape((state_rows, state_rows)),
            shape((LAYERS, rank * samples, state_rows)),
            shape((LAYERS, lin_rows, state_rows)),
            shape(fm_weight.shape),
            shape(fm_gain.shape, F32),
        ),
        table_host.reshape(1, tables),
        jnp.pad(jnp.transpose(fm_proj, (0, 2, 1)), ((0, 0), (0, proj_rows - rank), (0, 0))),
        lin_weight,
        fm_weight,
        fm_gain,
        after=(pooled,),
        flops=2 * 2 * flat_size * flat_size * fm_weight.shape[2],
    )
    flat_shape = shape((locals_, samples, flat_size))
    state, flat = call(
        first_layer,
        (shape((state_rows, width)), flat_shape),
        moved.reshape(state_rows, width),
        place,
        proj,
        gain,
    )
    for layer in range(LAYERS):
        gathered = exchange(flat, "local").reshape(locals_ * samples, flat_size)
        columns = call(
            lambda *refs, layer=layer: map_columns(layer, *refs),
            shape((locals_ * samples, fm_weight.shape[2])),
            gathered,
            weight,
        )
        mixed = exchange(columns.reshape(locals_, samples, -1), "local")
        if layer + 1 < LAYERS:
            state, flat = call(
                lambda *refs, layer=layer: next_layer(layer, *refs),
                (shape((state_rows, width)), flat_shape),
                mixed,
                state,
                lin,
                out_gain,
                proj,
                gain,
            )
        else:
            state = call(
                lambda *refs, layer=layer: last_state(layer, *refs),
                shape((state_rows, width)),
                mixed,
                state,
                lin,
                out_gain,
            )
    return state.reshape(samples, tables, width)


def solution(mesh):
    placed = (
        P(None, "local", "hst", None),
        P("hst", None, "local"),
        P(),
        P(),
        P(),
        P(),
        P(None, None, "local"),
        P(),
        P(),
        P(),
    )
    return jax.shard_map(
        shards,
        mesh=mesh,
        in_specs=placed,
        out_specs=P(("hst", "local"), None, None),
        check_vma=False,
    )
```

time: 215 us -> 111 us (0.52)
  waiting for transfers between devices: 47.3 us -> 10.7 us
  blocking collectives: 89.6 us -> 54.4 us
  between operations: 13.7 us -> 0.16 us
  Pallas kernels: 0 us -> 13.1 us
  local copies, waits for them, and re-layouts: 22.8 us -> 10.2 us
  other arithmetic: 9.32 us -> 0 us
  matrix products: 6.88 us -> 0 us
  starting transfers between devices: 24.1 us -> 21.8 us
    unnamed x2 -> x0, waiting for transfers between devices: 37.1 us -> none
    all_gather x2 -> x0, blocking collectives: 28.5 us -> none  [wukong_layer(): lax.all_gather(flat, 'local', axis=0, tiled=True)]
    gather x3 -> x0, local copies, waits for them, and re-layouts: 15.4 us -> none  [the longest x1 14.1 us: shards(): bags = jnp.take(bag_rows, owner_order, axis=0).astype(jnp.bfloat16)]
    pallas_call x0 -> x10, Pallas kernels: none -> 13.1 us  [call(): pl.pallas_call(kernel, out_shape=out_shape, in_specs=[pl.BlockSpec(memory...]
    dot_general x7 -> x0, matrix products: 6.88 us -> none  [the longest x2 4.92 us: wukong_layer(): jnp.dot(lax.all_gather(flat, 'local', axis=0, tiled=True), weight, prefer...]
    all_to_all x1 -> x5, blocking collectives: 61.1 us -> 54.4 us  [exchange(): return lax.all_to_all(value, axis, 0, 0, tiled=False)]
    convert_element_type x7 -> x0, other arithmetic: 4.93 us -> none  [the longest x1 3.61 us: shards(): bags = jnp.take(bag_rows, owner_order, axis=0).astype(jnp.bfloat16)]
    unnamed x18 -> x35, local copies, waits for them, and re-layouts: 5.78 us -> 10.2 us
  transfers between devices with their start and end apart: 4 -> 2, of which waited for: 3 -> 2; matrix products, arithmetic and copies ran while one was open for 10% -> 0% of each run, Pallas kernels for 0% -> 6%
where the time goes in v2:
time: 111 us; the launch traced here: 110 us
  blocking collectives  54.4 us (49%)
  starting transfers between devices  21.8 us (20%)
  Pallas kernels  13.1 us (12%)
  waiting for transfers between devices  10.7 us (10%)
  local copies, waits for them, and re-layouts  10.2 us (9%)
    all_to_all x5, blocking collectives, exchange(): return lax.all_to_all(value, axis, 0, 0, tiled=False)  54.4 us
    all_to_all x2, starting transfers between devices, exchange(): return lax.all_to_all(value, axis, 0, 0, tiled=False)  21.8 us
    pallas_call x10, Pallas kernels, call(): pl.pallas_call(kernel, out_shape=out_shape, in_specs=[pl.BlockSpec(memory...  13.1 us
    all_to_all x2, waiting for transfers between devices, exchange(): return lax.all_to_all(value, axis, 0, 0, tiled=False)  10.7 us
    unnamed x35, local copies, waits for them, and re-layouts  10.2 us
  transfers between devices with their start and end apart: 2, of which 2 were waited for; matrix products, arithmetic and copies ran while one was open for 0% of the time, Pallas kernels for 6%

profile of v2, /device:TPU:1, one launch (start us, length us, event | category | flops | bytes accessed | tf_op | source)
XLA Modules:
  0.0 110.4 jit_solution(15482018130399974694)
XLA Ops:
  0.0 0.0 copy-start.6
  0.0 0.8 copy-done.6
  0.8 0.7 copy-done.8
  1.4 0.0 copy-start.9
  1.4 0.7 copy-done.9
  2.1 0.9 shard_map.100.after_ref
  3.0 17.1 %all-to-all-start = ((f32[64,1,256]{2,1,0:T(1,128)}), f32[64,1,256]{2,1,0:T(1,128)S(1)}, u32[]{:S(2)}, u32[]{:S(2)}) async-start(f32[64,1,256]{2,1,0:T(1,128)} %shard_map.100.after_ref), calls=%async_computation | async-start | bytes 131072 | tf_op jit(solution)/shard_map/all_to_all | solution.py:239
  20.1 0.0 copy-start.12
  20.1 1.2 %copy-done.12 = s32[1,4096,64]{1,2,0:T(8,128)S(1)} copy-done((s32[1,4096,64]{1,2,0:T(8,128)S(1)}, s32[1,4096,64]{1,2,0:T(8,128)}, u32[]{:S(2)}) %copy-start.12) | copy-done | bytes 1048600
  21.3 0.0 copy-start.13
  21.3 0.7 copy-done.13
  22.1 0.0 copy-start.16
  22.1 0.0 copy-start.10
  22.1 0.0 copy-start.14
  22.1 0.0 copy-start.15
  22.1 2.4 %shard_map.101.ordered_ref = bf16[8,64,512]{2,1,0:T(8,128)(2,1)S(1)} custom-call(f32[64,1,256]{2,1,0:T(1,128)} %shard_map.100.after_ref, s32[64,4096]{1,0:T(8,128)S(1)} %bitcast.28, s32[32,128]{1,0:T(8,128)S(1)} %bitcast.29), custom_call_target="tpu_custom_call" | custom-call | flops 603979776 | bytes 1064960 | tf_op jit(solution)/shard_map/pallas_call | solution.py:226
  24.5 6.7 %all-to-all-done.arrived_ref = f32[64,1,256]{2,1,0:T(1,128)S(1)} async-done(((f32[64,1,256]{2,1,0:T(1,128)}), f32[64,1,256]{2,1,0:T(1,128)S(1)}, u32[]{:S(2)}, u32[]{:S(2)}) %all-to-all-start) | async-done | bytes 65568 | tf_op jit(solution)/shard_map/all_to_all | solution.py:239
  31.2 0.1 shard_map.102
  31.3 18.4 %all_to_all.35 = bf16[8,64,768]{2,1,0:T(8,128)(2,1)S(1)} all-to-all(bf16[8,64,768]{2,1,0:T(8,128)(2,1)S(1)} %shard_map.102), channel_id=1, replica_groups=mesh['hst'=64,'local'=8] {'local'}, dimensions={0} | all-to-all | bytes 1572864 | tf_op jit(solution)/shard_map/all_to_all | solution.py:239
  49.7 1.1 shard_map.103.after_ref
  50.7 4.6 %all-to-all-start.2 = ((bf16[64,8,256]{2,1,0:T(8,128)(2,1)}), bf16[64,8,256]{2,1,0:T(8,128)(2,1)S(1)}, u32[]{:S(2)}, u32[]{:S(2)}) async-start(bf16[64,8,256]{2,1,0:T(8,128)(2,1)} %bitcast.7), calls=%async_computation.2 | async-start | bytes 524288 | tf_op jit(solution)/shard_map/all_to_all | solution.py:239
  55.4 0.0 copy-done.16
  55.4 0.0 copy-done.10
  55.4 0.0 copy-done.14
  55.4 0.0 copy-done.15
  55.4 0.0 copy-start.11
  55.5 1.9 %copy-done.11 = bf16[2,768,1024]{2,1,0:T(8,128)(2,1)S(1)} copy-done((bf16[2,768,1024]{2,1,0:T(8,128)(2,1)S(1)}, bf16[2,768,1024]{2,1,0:T(8,128)(2,1)}, u32[]{:S(2)}) %copy-start.11) | copy-done | bytes 3145752
  57.3 0.0 copy-start.7
  57.3 4.2 %shard_map.104 = (bf16[512,512]{1,0:T(8,128)(2,1)S(1)}, bf16[2,96,512]{2,1,0:T(8,128)(2,1)S(1)}, bf16[2,256,512]{2,1,0:T(8,128)(2,1)S(1)}, bf16[2,768,1024]{2,1,0:T(8,128)(2,1)S(1)}, f32[2,768]{1,0:T(2,128)S(1)}) custom-call(bf16[512,256]{1,0:T(8,128)(2,1)} %shard_map.103.after_ref, s32[1,64]{1,0:T(1,128)S(1)} %bitcast.27, ...), custom_call_target="tpu_custom_call" | custom-call | flops 2415919104 | bytes 3164416 | tf_op jit(solution)/shard_map/pallas_call | solution.py:226
  61.6 0.0 copy-start
  61.6 0.8 copy-done
  62.4 0.0 copy-start.2
  62.4 0.7 copy-done.2
  63.1 0.8 copy-done.4
  63.9 4.0 %all-to-all-done.2 = bf16[64,8,256]{2,1,0:T(8,128)(2,1)S(1)} async-done(((bf16[64,8,256]{2,1,0:T(8,128)(2,1)}), bf16[64,8,256]{2,1,0:T(8,128)(2,1)S(1)}, u32[]{:S(2)}, u32[]{:S(2)}) %all-to-all-start.2) | async-done | bytes 262176 | tf_op jit(solution)/shard_map/all_to_all | solution.py:239
  67.9 1.0 copy-done.3
  68.9 1.0 copy-done.5
  69.9 1.1 %shard_map.105 = (bf16[512,256]{1,0:T(8,128)(2,1)S(1)}, bf16[8,8,768]{2,1,0:T(8,128)(2,1)S(1)}) custom-call(bf16[512,256]{1,0:T(8,128)(2,1)S(1)} %bitcast.19, bf16[512,512]{1,0:T(8,128)(2,1)S(1)} %copy-done.5, bf16[2,96,512]{2,1,0:T(8,128)(2,1)S(1)} %copy-done.3, f32[2,768]{1,0:T(2,128)S(1)} %get-tuple-element.16.gain_ref.refs_5_), custom_call_target="tpu_custom_call" | custom-call | bytes 989184 | tf_op jit(solution)/shard_map/pallas_call | solution.py:226
  71.0 10.8 %all_to_all.36 = bf16[8,8,768]{2,1,0:T(8,128)(2,1)S(1)} all-to-all(bf16[8,8,768]{2,1,0:T(8,128)(2,1)S(1)} %get-tuple-element.17), channel_id=1, replica_groups=mesh['hst'=64,'local'=8] {'local'}, dimensions={0} | all-to-all | bytes 196608 | tf_op jit(solution)/shard_map/all_to_all | solution.py:239
  81.9 0.4 shard_map.106
  82.2 8.5 %all_to_all.37.refs_0_ = bf16[8,8,1024]{2,1,0:T(8,128)(2,1)S(1)} all-to-all(bf16[8,8,1024]{2,1,0:T(8,128)(2,1)S(1)} %bitcast.21), channel_id=1, replica_groups=mesh['hst'=64,'local'=8] {'local'}, dimensions={0} | all-to-all | bytes 262144 | tf_op jit(solution)/shard_map/all_to_all | solution.py:239
  90.7 0.0 copy-done.7
  90.7 0.0 copy-done.1
  90.7 1.1 %shard_map.107 = (bf16[512,256]{1,0:T(8,128)(2,1)S(1)}, bf16[8,8,768]{2,1,0:T(8,128)(2,1)S(1)}) custom-call(bf16[8,8,1024]{2,1,0:T(8,128)(2,1)S(1)} %all_to_all.37.refs_0_, bf16[512,256]{1,0:T(8,128)(2,1)S(1)} %get-tuple-element.19.refs_1_, bf16[2,256,512]{2,1,0:T(8,128)(2,1)S(1)} %copy-done.1, f32[2,256]{1,0:T(2,128)S(1)} %copy-done.7, ...), custom_call_target="tpu_custom_call" | custom-call | bytes 1122304 | tf_op jit(solution)/shard_map/pallas_call | solution.py:226
  91.8 8.2 %all_to_all.38 = bf16[8,8,768]{2,1,0:T(8,128)(2,1)S(1)} all-to-all(bf16[8,8,768]{2,1,0:T(8,128)(2,1)S(1)} %get-tuple-element.21), channel_id=1, replica_groups=mesh['hst'=64,'local'=8] {'local'}, dimensions={0} | all-to-all | bytes 196608 | tf_op jit(solution)/shard_map/all_to_all | solution.py:239
  100.1 0.4 shard_map.108
  100.5 8.5 %all_to_all.39.refs_0_ = bf16[8,8,1024]{2,1,0:T(8,128)(2,1)S(1)} all-to-all(bf16[8,8,1024]{2,1,0:T(8,128)(2,1)S(1)} %bitcast.20), channel_id=1, replica_groups=mesh['hst'=64,'local'=8] {'local'}, dimensions={0} | all-to-all | bytes 262144 | tf_op jit(solution)/shard_map/all_to_all | solution.py:239
  108.9 1.4 %shard_map.109 = bf16[512,256]{1,0:T(8,128)(2,1)} custom-call(bf16[8,8,1024]{2,1,0:T(8,128)(2,1)S(1)} %all_to_all.39.refs_0_, bf16[512,256]{1,0:T(8,128)(2,1)S(1)} %get-tuple-element.22.refs_1_, bf16[2,256,512]{2,1,0:T(8,128)(2,1)S(1)} %copy-done.1, f32[2,256]{1,0:T(2,128)S(1)} %copy-done.7), custom_call_target="tpu_custom_call" | custom-call | bytes 919552 | tf_op jit(solution)/shard_map/pallas_call | solution.py:226
  (7 shorter events, 0.0 us)
Async XLA Ops:
  0.0 0.8 copy-start.6
  0.8 0.7 copy-start.8
  1.4 0.7 copy-start.9
  3.0 28.2 %all-to-all-start = ((f32[64,1,256]{2,1,0:T(1,128)}), f32[64,1,256]{2,1,0:T(1,128)S(1)}, u32[]{:S(2)}, u32[]{:S(2)}) async-start(f32[64,1,256]{2,1,0:T(1,128)} %shard_map.100.after_ref), calls=%async_computation | async-start | bytes 131072 | tf_op jit(solution)/shard_map/all_to_all | solution.py:239
  20.1 1.2 %copy-start.12 = (s32[1,4096,64]{1,2,0:T(8,128)S(1)}, s32[1,4096,64]{1,2,0:T(8,128)}, u32[]{:S(2)}) copy-start(s32[1,4096,64]{1,2,0:T(8,128)} %param.11) | copy-start | bytes 3145732
  21.3 0.7 copy-start.13
  22.1 33.3 %copy-start.16 = (bf16[2,64,12]{1,0,2:T(2,128)(2,1)S(1)}, bf16[2,64,12]{1,0,2:T(2,128)(2,1)}, u32[]{:S(2)}) copy-start(bf16[2,64,12]{1,0,2:T(2,128)(2,1)} %param.15) | copy-start | bytes 9220
  22.1 33.4 %copy-start.10 = (s32[64]{0:T(128)S(1)}, s32[64]{0:T(128)}, u32[]{:S(2)}) copy-start(s32[64]{0:T(128)} %param.12) | copy-start | bytes 772
  22.1 33.4 %copy-start.14 = (bf16[2,32,64]{2,1,0:T(8,128)(2,1)S(1)}, bf16[2,32,64]{2,1,0:T(8,128)(2,1)}, u32[]{:S(2)}) copy-start(bf16[2,32,64]{2,1,0:T(8,128)(2,1)} %lin_ref.1) | copy-start | bytes 24580
  22.1 33.4 %copy-start.15 = (f32[2,768]{1,0:T(2,128)S(1)}, f32[2,768]{1,0:T(2,128)}, u32[]{:S(2)}) copy-start(f32[2,768]{1,0:T(2,128)} %gain_ref.1) | copy-start | bytes 18436
  50.7 17.1 %all-to-all-start.2 = ((bf16[64,8,256]{2,1,0:T(8,128)(2,1)}), bf16[64,8,256]{2,1,0:T(8,128)(2,1)S(1)}, u32[]{:S(2)}, u32[]{:S(2)}) async-start(bf16[64,8,256]{2,1,0:T(8,128)(2,1)} %bitcast.7), calls=%async_computation.2 | async-start | bytes 524288 | tf_op jit(solution)/shard_map/all_to_all | solution.py:239
  55.4 1.9 %copy-start.11 = (bf16[2,768,1024]{2,1,0:T(8,128)(2,1)S(1)}, bf16[2,768,1024]{2,1,0:T(8,128)(2,1)}, u32[]{:S(2)}) copy-start(bf16[2,768,1024]{2,1,0:T(8,128)(2,1)} %weight_ref.1) | copy-start | bytes 9437188
  57.3 33.4 %copy-start.7 = (f32[2,256]{1,0:T(2,128)S(1)}, f32[2,256]{1,0:T(2,128)}, u32[]{:S(2)}) copy-start(f32[2,256]{1,0:T(2,128)} %refs_3_.3) | copy-start | bytes 6148
  61.6 0.8 copy-start
  62.4 0.7 copy-start.2
  63.1 0.8 copy-start.4
  67.9 22.9 %copy-start.1 = (bf16[2,256,512]{2,1,0:T(8,128)(2,1)S(1)}, bf16[2,256,512]{2,1,0:T(8,128)(2,1)}, u32[]{:S(2)}) copy-start(bf16[2,256,512]{2,1,0:T(8,128)(2,1)} %copy-done) | copy-start | bytes 1572868
  67.9 1.0 copy-start.3
  68.9 1.0 copy-start.5

commit v3 on v2

v3 whole, which is shorter than its diff:
```python
import jax
import jax.numpy as jnp
from jax import lax
from jax.experimental import pallas as pl
from jax.experimental.pallas import tpu as pltpu
from jax.sharding import PartitionSpec as P

LAYERS = 2
PACK = 4
LOW = 256
LANES = 128
SMALL, MIDDLE, LARGE = 40 << 20, 49 << 20, 60 << 20
F32 = jnp.float32
BF16 = jnp.bfloat16


def number(shape, axis):
    return lax.broadcasted_iota(jnp.int32, shape, axis)


def ones_where(condition):
    return jnp.where(condition, 1.0, 0.0).astype(BF16)


def matmul(a, b):
    return jnp.dot(a, b, preferred_element_type=F32)


def matmul_nt(a, b):
    return lax.dot_general(a, b, (((1,), (1,)), ((), ())), preferred_element_type=F32)


def matmul_tn(a, b):
    return lax.dot_general(a, b, (((0,), (0,)), ((), ())), preferred_element_type=F32)


def fetch(pairs, sems):
    copies = [pltpu.make_async_copy(source, target, sems.at[at]) for at, (source, target) in enumerate(pairs)]
    for copy in copies:
        copy.start()
    return copies


def pick_rows(host_hbm, slot_hbm, stored_hbm, out_ref, host_ref, slot_ref, stored_ref, sems):
    for copy in fetch([(host_hbm, host_ref), (slot_hbm, slot_ref), (stored_hbm, stored_ref)], sems):
        copy.wait()
    tables = stored_ref.shape[0]
    holder = ones_where(number((tables, tables), 0) == host_ref[...])
    slot = ones_where(number((tables, tables), 0) == slot_ref[...])
    chosen = matmul_nt(holder, slot).astype(BF16)
    out_ref[:, 0, :] = matmul(chosen, stored_ref[...])


def order_counts(counts_ref, order_ref, out_ref, packed_ref):
    rows, batch = counts_ref.shape
    targets, _, length = out_ref.shape
    words = rows // PACK
    high_count = batch // LOW
    order_rows = order_ref.shape[0]
    samples = 8
    word = counts_ref[0:words, :]
    for k in range(1, PACK):
        word = word + (counts_ref[k * words : (k + 1) * words, :] << (2 * k))
    word = word.astype(F32).astype(BF16)
    for high in range(high_count):
        packed_ref[high * words : (high + 1) * words, :] = word[:, high * LOW : (high + 1) * LOW]
    order = order_ref[...]
    parts = jnp.concatenate([order >> 8, order & (LOW - 1)], axis=0).astype(F32).astype(BF16)
    for target in range(targets):
        m = number((LANES, length), 1)
        row = (m // samples) * (targets * samples) + target * samples + m % samples
        found = matmul(parts, ones_where(number((LANES, length), 0) == row % LANES))
        m = number((2 * order_rows, length), 1)
        row = (m // samples) * (targets * samples) + target * samples + m % samples
        found = jnp.where(
            number((2 * order_rows, length), 0) % order_rows == row // LANES, found, 0.0
        )
        high_part = jnp.sum(found[:order_rows], axis=0, keepdims=True).astype(jnp.int32)
        low_part = jnp.sum(found[order_rows:], axis=0, keepdims=True).astype(jnp.int32)
        picked = matmul(packed_ref[...], ones_where(number((LOW, length), 0) == low_part))
        value = jnp.zeros((words, length), F32)
        for high in range(high_count):
            value = value + jnp.where(
                high_part == high, picked[high * words : (high + 1) * words, :], 0.0
            )
        value = value.astype(jnp.int32)
        for k in range(PACK):
            out_ref[target, k * words : (k + 1) * words, :] = (
                ((value >> (2 * k)) & 3).astype(F32).astype(BF16)
            )


def join_table(arrived_ref, ordered_ref, out_ref):
    length = ordered_ref.shape[2]
    table = arrived_ref[:, 0, :].astype(BF16)
    for target in range(out_ref.shape[0]):
        out_ref[target, :, :length] = ordered_ref[target]
        out_ref[target, :, length:] = table


def pool(both_ref, out_ref):
    length = out_ref.shape[0]
    out_ref[...] = matmul_tn(both_ref[:, :length], both_ref[:, length:]).astype(BF16)


def per_sample(matrix, samples):
    few, tables = matrix.shape
    rows, columns = few * samples, samples * tables
    tall = ones_where(number((rows, few), 0) // samples == number((rows, few), 1))
    wide = ones_where(number((tables, columns), 1) % tables == number((tables, columns), 0))
    values = matmul(matmul(tall, matrix).astype(BF16), wide)
    own = number((rows, columns), 0) % samples == number((rows, columns), 1) // tables
    return jnp.where(own, values, 0.0).astype(BF16)


def norm_rows(values, gain):
    mean = jnp.mean(values, axis=-1, keepdims=True)
    centered = values - mean
    spread_ = jnp.mean(centered * centered, axis=-1, keepdims=True)
    return centered * lax.rsqrt(spread_ + 1e-05) * gain


def gain_blocks(gain, rank):
    flat = gain.shape[1]
    tables = flat // rank
    lane = number((16, flat), 1)
    own = lane % rank == number((16, flat), 0)
    to_table = ones_where(
        number((flat, LANES), 0) // rank == number((flat, LANES), 1) % tables
    )
    total = jnp.zeros((16, LANES), F32)
    for _ in range(3):
        part = gain.astype(BF16).astype(F32)
        gain = gain - part
        total = total + matmul(jnp.where(own, part, 0.0).astype(BF16), to_table)
    first = number((1, LANES), 1) < tables
    return [
        jnp.where(first, total[k : k + 1], total[k + 1 : k + 2]) for k in range(0, rank, 2)
    ]


def interactions(state, proj_ref, gain_ref, layer, flat_ref):
    rows = state.shape[0]
    samples = flat_ref.shape[1]
    rank, _, tables = proj_ref.shape
    proj = jnp.concatenate(
        [proj_ref[...].astype(F32)[:, layer, :], jnp.zeros((16 - rank, tables), F32)], axis=0
    ).astype(BF16)
    proj = per_sample(proj, samples)[: rank * samples]
    gain = jnp.concatenate(gain_blocks(gain_ref[layer : layer + 1, :], rank), axis=1)
    inner = matmul(proj, state).astype(BF16)
    inter = matmul_nt(inner, state)
    own = number(inter.shape, 0) % samples == number(inter.shape, 1) // tables
    inter = jnp.where(own, inter, 0.0)
    while inter.shape[1] > LANES:
        half = inter.shape[1] // 2
        inter = inter[:, :half] + inter[:, half:]
    inter = inter + pltpu.roll(inter, tables, 1)
    first = number((samples, LANES), 1) < tables
    flat = jnp.concatenate(
        [
            jnp.where(first, inter[at : at + samples], inter[at + samples : at + 2 * samples])
            for at in range(0, inter.shape[0], 2 * samples)
        ],
        axis=1,
    )
    flat = norm_rows(flat, gain).astype(BF16)
    for target in range(flat_ref.shape[0]):
        flat_ref[target] = flat


def first_layer(
    weight_hbm, moved_ref, host_ref, proj_ref, gain_ref, state_ref, flat_ref, weight_ref, sems
):
    copies = fetch([(weight_hbm.at[0], weight_ref.at[0])], sems)
    rows = state_ref.shape[0]
    tables = host_ref.shape[1]
    samples = rows // tables
    holder = ones_where(number((tables, tables), 0) == host_ref[...])
    tall = ones_where(number((rows, tables), 0) % tables == number((rows, tables), 1))
    wide = ones_where(number((tables, rows), 1) // samples == number((tables, rows), 0))
    place = matmul(matmul_nt(tall, holder).astype(BF16), wide)
    own = number((rows, rows), 0) // tables == number((rows, rows), 1) % samples
    place = jnp.where(own, place, 0.0).astype(BF16)
    state = matmul(place, moved_ref[...]).astype(BF16)
    state_ref[...] = state
    interactions(state, proj_ref, gain_ref, 0, flat_ref)
    copies[0].wait()


def map_columns(layer, rank, flat_ref, weight_ref, out_ref):
    flat = flat_ref.shape[1]
    tables = flat // rank
    row = number((flat, flat), 0)
    order = ones_where((row % tables) * rank + row // tables == number((flat, flat), 1))
    out_ref[...] = matmul(
        matmul(flat_ref[...], order).astype(BF16), weight_ref[min(layer, weight_ref.shape[0] - 1)]
    ).astype(BF16)


def next_state(layer, mixed_ref, state_ref, lin_ref, scale_ref):
    rows, width = state_ref.shape
    sources, samples, part = mixed_ref.shape
    made = sources * part // width
    tables = rows // samples
    mixed = jnp.concatenate(
        [
            mixed_ref[source, :, start : start + width].astype(F32)
            for source in range(sources)
            for start in range(0, part, width)
        ],
        axis=0,
    ).astype(BF16)
    row = number((made * samples, made * samples), 0)
    turn = ones_where(
        (row % made) * samples + row // made == number((made * samples, made * samples), 1)
    )
    mixed = matmul(turn, mixed)
    joined = []
    for sample in range(samples):
        joined.append(mixed[sample * made : (sample + 1) * made])
        joined.append(
            matmul(lin_ref[layer], state_ref[sample * tables : (sample + 1) * tables, :])
        )
    joined = jnp.concatenate(joined, axis=0) + state_ref[...].astype(F32)
    return norm_rows(joined, scale_ref[layer : layer + 1, :]).astype(BF16)


def next_layer(
    layer, mixed_ref, old_ref, lin_ref, scale_ref, proj_ref, gain_ref, state_ref, flat_ref
):
    state = next_state(layer, mixed_ref, old_ref, lin_ref, scale_ref)
    state_ref[...] = state
    interactions(state, proj_ref, gain_ref, layer + 1, flat_ref)


def last_state(layer, mixed_ref, old_ref, lin_ref, scale_ref, out_ref):
    out_ref[...] = next_state(layer, mixed_ref, old_ref, lin_ref, scale_ref)


def call(kernel, out_shape, *args, own=(), scratch=(), flops=0, limit=SMALL):
    moved = sum(a.size * a.dtype.itemsize for a in (*own, *args))
    return pl.pallas_call(
        kernel,
        out_shape=out_shape,
        in_specs=[pl.BlockSpec(memory_space=pl.ANY)] * len(own)
        + [pl.BlockSpec(memory_space=pltpu.VMEM)] * len(args),
        out_specs=jax.tree.map(lambda _: pl.BlockSpec(memory_space=pltpu.VMEM), out_shape),
        scratch_shapes=list(scratch),
        compiler_params=pltpu.CompilerParams(vmem_limit_bytes=limit),
        cost_estimate=pl.CostEstimate(flops=flops, bytes_accessed=moved, transcendentals=0),
    )(*own, *args)


def exchange(value, axis):
    return lax.all_to_all(value, axis, 0, 0, tiled=False)


def shards(
    checkpoint,
    counts,
    table_host,
    stored_slot,
    owner_order,
    fm_proj,
    fm_weight,
    fm_gain,
    lin_weight,
    out_gain,
):
    hosts = lax.axis_size("hst")
    locals_ = lax.axis_size("local")
    width = checkpoint.shape[-1]
    tables = table_host.shape[0]
    batch = owner_order.shape[0]
    samples = batch // (hosts * locals_)
    rows = counts.shape[2]
    length = hosts * samples
    state_rows = tables * samples
    rank = fm_proj.shape[2]
    flat_size = tables * rank

    def shape(dims, dtype=BF16):
        return jax.ShapeDtypeStruct(dims, dtype)

    def fetched(*arrays):
        return [pltpu.VMEM(a.shape, a.dtype) for a in arrays]

    host = table_host.reshape(1, tables)
    picked = (host, stored_slot.reshape(1, tables), checkpoint.reshape(tables, width))
    outgoing = call(
        pick_rows,
        shape((tables, 1, width), F32),
        own=picked,
        scratch=[*fetched(*picked), pltpu.SemaphoreType.DMA((3,))],
        limit=LARGE,
    )
    arrived = exchange(outgoing, "hst")
    ordered = call(
        order_counts,
        shape((locals_, rows, length)),
        jnp.transpose(counts[0]),
        owner_order.reshape(batch // LANES, LANES),

        scratch=[pltpu.VMEM((batch // LOW * (rows // PACK), LOW), BF16)],
        flops=2 * batch * (LOW * LOW + 64 * LANES),
    )
    both = exchange(
        call(join_table, shape((locals_, rows, length + width)), arrived, ordered), "local"
    )
    pooled = call(pool, shape((length, width)), both.reshape(locals_ * rows, length + width))
    moved = exchange(pooled.reshape(hosts, samples, width), "hst")

    made = (
        shape((state_rows, width)),
        shape((locals_, samples, flat_size)),
    )
    proj = jnp.transpose(fm_proj, (2, 0, 1))
    state, flat, weight = call(
        first_layer,
        (*made, shape((1, *fm_weight.shape[1:]))),
        moved.reshape(state_rows, width),
        host,
        proj,
        fm_gain,
        own=(fm_weight,),
        scratch=[pltpu.SemaphoreType.DMA((1,))],
        limit=MIDDLE,
    )
    for layer in range(LAYERS):
        gathered = exchange(flat, "local").reshape(locals_ * samples, flat_size)
        columns = call(
            lambda *refs, layer=layer: map_columns(layer, rank, *refs),
            shape((locals_ * samples, fm_weight.shape[2])),
            gathered,
            fm_weight if layer else weight,
        )
        mixed = exchange(columns.reshape(locals_, samples, -1), "local")
        if layer + 1 < LAYERS:
            state, flat = call(
                lambda *refs, layer=layer: next_layer(layer, *refs),
                made,
                mixed,
                state,
                lin_weight,
                out_gain,
                proj,
                fm_gain,
            )
        else:
            state = call(
                lambda *refs, layer=layer: last_state(layer, *refs),
                shape((state_rows, width)),
                mixed,
                state,
                lin_weight,
                out_gain,
            )
    return state.reshape(samples, tables, width)


def solution(mesh):
    placed = (
        P(None, "local", "hst", None),
        P("hst", None, "local"),
        P(),
        P(),
        P(),
        P(),
        P(None, None, "local"),
        P(),
        P(),
        P(),
    )
    return jax.shard_map(
        shards,
        mesh=mesh,
        in_specs=placed,
        out_specs=P(("hst", "local"), None, None),
        check_vma=False,
    )
```

time: 111 us -> 107 us (0.964)
  blocking collectives: 54.4 us -> 71.2 us
  local copies, waits for them, and re-layouts: 10.2 us -> 1.97 us
  starting transfers between devices: 21.8 us -> 17.1 us
  waiting for transfers between devices: 10.7 us -> 6.71 us
  Pallas kernels: 13.1 us -> 9.58 us
    all_to_all x5 -> x6, blocking collectives: 54.4 us -> 71.2 us  [exchange(): return lax.all_to_all(value, axis, 0, 0, tiled=False)]
    unnamed x35 -> x16, local copies, waits for them, and re-layouts: 10.2 us -> 1.97 us
    all_to_all x2 -> x1, starting transfers between devices: 21.8 us -> 17.1 us  [exchange(): return lax.all_to_all(value, axis, 0, 0, tiled=False)]
    all_to_all x2 -> x1, waiting for transfers between devices: 10.7 us -> 6.71 us  [exchange(): return lax.all_to_all(value, axis, 0, 0, tiled=False)]
    pallas_call x10 -> x9, Pallas kernels: 13.1 us -> 9.58 us  [call(): pl.pallas_call(kernel, out_shape=out_shape, in_specs=[pl.BlockSpec(memory...]
  transfers between devices with their start and end apart: 2 -> 1, of which waited for: 2 -> 1; matrix products, arithmetic and copies ran while one was open for 0% -> 0% of each run, Pallas kernels for 6% -> 2%
where the time goes in v3:
time: 107 us
  blocking collectives  71.2 us (67%)
  starting transfers between devices  17.1 us (16%)
  Pallas kernels  9.58 us (9%)
  waiting for transfers between devices  6.71 us (6%)
  local copies, waits for them, and re-layouts  1.97 us (2%)
    all_to_all x6, blocking collectives, exchange(): return lax.all_to_all(value, axis, 0, 0, tiled=False)  71.2 us
    all_to_all x1, starting transfers between devices, exchange(): return lax.all_to_all(value, axis, 0, 0, tiled=False)  17.1 us
    pallas_call x9, Pallas kernels, call(): pl.pallas_call(kernel, out_shape=out_shape, in_specs=[pl.BlockSpec(memory...  9.58 us
    all_to_all x1, waiting for transfers between devices, exchange(): return lax.all_to_all(value, axis, 0, 0, tiled=False)  6.71 us
  transfers between devices with their start and end apart: 1, of which 1 were waited for; matrix products, arithmetic and copies ran while one was open for 0% of the time, Pallas kernels for 2%

profile of v3, /device:TPU:1, one launch (start us, length us, event | category | flops | bytes accessed | tf_op | source)
XLA Modules:
  0.0 106.7 jit_solution(6816582753963687724)
XLA Ops:
  0.0 1.7 %shard_map.100 = f32[64,1,256]{2,1,0:T(1,128)} custom-call(s32[1,64]{1,0:T(1,128)} %bitcast.25, s32[1,64]{1,0:T(1,128)} %bitcast.30, bf16[64,256]{1,0:T(8,128)(2,1)} %bitcast.29), custom_call_target="tpu_custom_call" | custom-call | bytes 33280 | tf_op jit(solution)/shard_map/pallas_call | solution.py:243
  1.7 17.1 %all-to-all-start = ((f32[64,1,256]{2,1,0:T(1,128)}), f32[64,1,256]{2,1,0:T(1,128)S(1)}, u32[]{:S(2)}, u32[]{:S(2)}) async-start(f32[64,1,256]{2,1,0:T(1,128)} %shard_map.100), calls=%async_computation | async-start | bytes 131072 | tf_op jit(solution)/shard_map/all_to_all | solution.py:256
  18.9 0.0 copy-start.6
  18.9 1.2 %copy-done.6 = s32[1,4096,64]{1,2,0:T(8,128)S(1)} copy-done((s32[1,4096,64]{1,2,0:T(8,128)S(1)}, s32[1,4096,64]{1,2,0:T(8,128)}, u32[]{:S(2)}) %copy-start.6) | copy-done | bytes 1048600
  20.1 0.0 copy-start.7
  20.1 0.7 copy-done.7
  20.8 0.0 copy-start.2
  20.8 0.0 copy-start.3
  20.8 0.0 copy-start.5
  20.8 2.4 %shard_map.101.ordered_ref = bf16[8,64,512]{2,1,0:T(8,128)(2,1)S(1)} custom-call(s32[64,4096]{1,0:T(8,128)S(1)} %bitcast.27, s32[32,128]{1,0:T(8,128)S(1)} %bitcast.28), custom_call_target="tpu_custom_call" | custom-call | flops 603979776 | bytes 1064960 | tf_op jit(solution)/shard_map/pallas_call | solution.py:243
  23.2 6.7 %all-to-all-done.arrived_ref = f32[64,1,256]{2,1,0:T(1,128)S(1)} async-done(((f32[64,1,256]{2,1,0:T(1,128)}), f32[64,1,256]{2,1,0:T(1,128)S(1)}, u32[]{:S(2)}, u32[]{:S(2)}) %all-to-all-start) | async-done | bytes 65568 | tf_op jit(solution)/shard_map/all_to_all | solution.py:256
  30.0 0.1 shard_map.102
  30.0 18.4 %all_to_all.35 = bf16[8,64,768]{2,1,0:T(8,128)(2,1)S(1)} all-to-all(bf16[8,64,768]{2,1,0:T(8,128)(2,1)S(1)} %shard_map.102), channel_id=1, replica_groups=mesh['hst'=64,'local'=8] {'local'}, dimensions={0} | all-to-all | bytes 1572864 | tf_op jit(solution)/shard_map/all_to_all | solution.py:256
  48.5 0.3 shard_map.103
  48.8 0.0 copy-start.1
  48.8 0.0 copy-start.4
  48.8 16.8 %all_to_all.36 = bf16[64,8,256]{2,1,0:T(8,128)(2,1)S(1)} all-to-all(bf16[64,8,256]{2,1,0:T(8,128)(2,1)S(1)} %bitcast.18), channel_id=1, replica_groups=mesh['hst'=64,'local'=8] {'hst'}, dimensions={0} | all-to-all | bytes 524288 | tf_op jit(solution)/shard_map/all_to_all | solution.py:256
  65.7 0.0 copy-done.2
  65.7 0.0 copy-done.3
  65.7 0.0 copy-done.5
  65.7 0.0 copy-start
  65.7 1.6 %shard_map.104 = (bf16[512,256]{1,0:T(8,128)(2,1)S(1)}, bf16[8,8,768]{2,1,0:T(8,128)(2,1)S(1)}, bf16[1,768,1024]{2,1,0:T(8,128)(2,1)S(1)}) custom-call(bf16[2,768,1024]{2,1,0:T(8,128)(2,1)} %refs_1_.1, bf16[512,256]{1,0:T(8,128)(2,1)S(1)} %bitcast.17, s32[1,64]{1,0:T(1,128)S(1)} %bitcast.26, bf16[12,2,64]{2,1,0:T(2,128)(2,1)S(1)} %bitcast.23, ...), custom_call_target="tpu_custom_call" | custom-call | bytes 3417344 | tf_op jit(solution)/shard_map/pallas_call | solution.py:243
  67.3 10.8 %all_to_all.37 = bf16[8,8,768]{2,1,0:T(8,128)(2,1)S(1)} all-to-all(bf16[8,8,768]{2,1,0:T(8,128)(2,1)S(1)} %get-tuple-element.10), channel_id=1, replica_groups=mesh['hst'=64,'local'=8] {'local'}, dimensions={0} | all-to-all | bytes 196608 | tf_op jit(solution)/shard_map/all_to_all | solution.py:256
  78.1 0.7 shard_map.105
  78.8 8.5 %all_to_all.38.refs_0_ = bf16[8,8,1024]{2,1,0:T(8,128)(2,1)S(1)} all-to-all(bf16[8,8,1024]{2,1,0:T(8,128)(2,1)S(1)} %bitcast.19), channel_id=1, replica_groups=mesh['hst'=64,'local'=8] {'local'}, dimensions={0} | all-to-all | bytes 262144 | tf_op jit(solution)/shard_map/all_to_all | solution.py:256
  87.3 0.0 copy-done.1
  87.3 0.0 copy-done.4
  87.3 1.0 shard_map.106
  88.3 8.2 %all_to_all.39 = bf16[8,8,768]{2,1,0:T(8,128)(2,1)S(1)} all-to-all(bf16[8,8,768]{2,1,0:T(8,128)(2,1)S(1)} %get-tuple-element.13), channel_id=1, replica_groups=mesh['hst'=64,'local'=8] {'local'}, dimensions={0} | all-to-all | bytes 196608 | tf_op jit(solution)/shard_map/all_to_all | solution.py:256
  96.5 0.0 copy-done
  96.5 0.7 shard_map.107
  97.2 8.5 %all_to_all.40.refs_0_ = bf16[8,8,1024]{2,1,0:T(8,128)(2,1)S(1)} all-to-all(bf16[8,8,1024]{2,1,0:T(8,128)(2,1)S(1)} %bitcast.20), channel_id=1, replica_groups=mesh['hst'=64,'local'=8] {'local'}, dimensions={0} | all-to-all | bytes 262144 | tf_op jit(solution)/shard_map/all_to_all | solution.py:256
  105.6 1.1 %shard_map.108 = bf16[512,256]{1,0:T(8,128)(2,1)} custom-call(bf16[8,8,1024]{2,1,0:T(8,128)(2,1)S(1)} %all_to_all.40.refs_0_, bf16[512,256]{1,0:T(8,128)(2,1)S(1)} %get-tuple-element.14.refs_1_, bf16[2,32,64]{2,1,0:T(8,128)(2,1)S(1)} %copy-done.1, f32[2,256]{1,0:T(2,128)S(1)} %copy-done.4), custom_call_target="tpu_custom_call" | custom-call | bytes 403456 | tf_op jit(solution)/shard_map/pallas_call | solution.py:243
Async XLA Ops:
  1.7 28.2 %all-to-all-start = ((f32[64,1,256]{2,1,0:T(1,128)}), f32[64,1,256]{2,1,0:T(1,128)S(1)}, u32[]{:S(2)}, u32[]{:S(2)}) async-start(f32[64,1,256]{2,1,0:T(1,128)} %shard_map.100), calls=%async_computation | async-start | bytes 131072 | tf_op jit(solution)/shard_map/all_to_all | solution.py:256
  18.9 1.2 %copy-start.6 = (s32[1,4096,64]{1,2,0:T(8,128)S(1)}, s32[1,4096,64]{1,2,0:T(8,128)}, u32[]{:S(2)}) copy-start(s32[1,4096,64]{1,2,0:T(8,128)} %param.11) | copy-start | bytes 3145732
  20.1 0.7 copy-start.7
  20.8 44.9 %copy-start.2 = (bf16[2,64,12]{1,0,2:T(2,128)(2,1)S(1)}, bf16[2,64,12]{1,0,2:T(2,128)(2,1)}, u32[]{:S(2)}) copy-start(bf16[2,64,12]{1,0,2:T(2,128)(2,1)} %param.15) | copy-start | bytes 9220
  20.8 44.9 %copy-start.3 = (f32[2,768]{1,0:T(2,128)S(1)}, f32[2,768]{1,0:T(2,128)}, u32[]{:S(2)}) copy-start(f32[2,768]{1,0:T(2,128)} %refs_5_.1) | copy-start | bytes 18436
  20.8 44.9 %copy-start.5 = (s32[64]{0:T(128)S(1)}, s32[64]{0:T(128)}, u32[]{:S(2)}) copy-start(s32[64]{0:T(128)} %param.12) | copy-start | bytes 772
  48.8 38.4 %copy-start.1 = (bf16[2,32,64]{2,1,0:T(8,128)(2,1)S(1)}, bf16[2,32,64]{2,1,0:T(8,128)(2,1)}, u32[]{:S(2)}) copy-start(bf16[2,32,64]{2,1,0:T(8,128)(2,1)} %refs_2_.3) | copy-start | bytes 24580
  48.8 38.4 %copy-start.4 = (f32[2,256]{1,0:T(2,128)S(1)}, f32[2,256]{1,0:T(2,128)}, u32[]{:S(2)}) copy-start(f32[2,256]{1,0:T(2,128)} %refs_3_.3) | copy-start | bytes 6148
  65.7 30.8 %copy-start = (bf16[2,768,1024]{2,1,0:T(8,128)(2,1)S(1)}, bf16[2,768,1024]{2,1,0:T(8,128)(2,1)}, u32[]{:S(2)}) copy-start(bf16[2,768,1024]{2,1,0:T(8,128)(2,1)} %refs_1_.1) | copy-start | bytes 9437188

commit v4 on v3

--- a/solution.py
+++ b/solution.py
@@ -9,6 +9,8 @@
 PACK = 4
 LOW = 256
 LANES = 128
+SIDE = 8
+FIRST, SECOND = (6, 4), (4, 4)
 SMALL, MIDDLE, LARGE = 40 << 20, 49 << 20, 60 << 20
 F32 = jnp.float32
 BF16 = jnp.bfloat16
@@ -41,11 +43,15 @@
     return copies
 
 
+def host_of(rank, start):
+    return (rank // SIDE + start[0]) % SIDE * SIDE + (rank % SIDE + start[1]) % SIDE
+
+
 def pick_rows(host_hbm, slot_hbm, stored_hbm, out_ref, host_ref, slot_ref, stored_ref, sems):
     for copy in fetch([(host_hbm, host_ref), (slot_hbm, slot_ref), (stored_hbm, stored_ref)], sems):
         copy.wait()
     tables = stored_ref.shape[0]
-    holder = ones_where(number((tables, tables), 0) == host_ref[...])
+    holder = ones_where(host_of(number((tables, tables), 0), FIRST) == host_ref[...])
     slot = ones_where(number((tables, tables), 0) == slot_ref[...])
     chosen = matmul_nt(holder, slot).astype(BF16)
     out_ref[:, 0, :] = matmul(chosen, stored_ref[...])
@@ -68,10 +74,10 @@
     parts = jnp.concatenate([order >> 8, order & (LOW - 1)], axis=0).astype(F32).astype(BF16)
     for target in range(targets):
         m = number((LANES, length), 1)
-        row = (m // samples) * (targets * samples) + target * samples + m % samples
+        row = host_of(m // samples, SECOND) * (targets * samples) + target * samples + m % samples
         found = matmul(parts, ones_where(number((LANES, length), 0) == row % LANES))
         m = number((2 * order_rows, length), 1)
-        row = (m // samples) * (targets * samples) + target * samples + m % samples
+        row = host_of(m // samples, SECOND) * (targets * samples) + target * samples + m % samples
         found = jnp.where(
             number((2 * order_rows, length), 0) % order_rows == row // LANES, found, 0.0
         )
@@ -92,7 +98,9 @@
 
 def join_table(arrived_ref, ordered_ref, out_ref):
     length = ordered_ref.shape[2]
-    table = arrived_ref[:, 0, :].astype(BF16)
+    rows = arrived_ref.shape[0]
+    place = ones_where(number((rows, rows), 0) == host_of(number((rows, rows), 1), FIRST))
+    table = matmul(place, arrived_ref[:, 0, :].astype(BF16)).astype(BF16)
     for target in range(out_ref.shape[0]):
         out_ref[target, :, :length] = ordered_ref[target]
         out_ref[target, :, length:] = table
@@ -176,7 +184,7 @@
     rows = state_ref.shape[0]
     tables = host_ref.shape[1]
     samples = rows // tables
-    holder = ones_where(number((tables, tables), 0) == host_ref[...])
+    holder = ones_where(host_of(number((tables, tables), 0), SECOND) == host_ref[...])
     tall = ones_where(number((rows, tables), 0) % tables == number((rows, tables), 1))
     wide = ones_where(number((tables, rows), 1) // samples == number((tables, rows), 0))
     place = matmul(matmul_nt(tall, holder).astype(BF16), wide)
@@ -252,8 +260,8 @@
     )(*own, *args)
 
 
-def exchange(value, axis):
-    return lax.all_to_all(value, axis, 0, 0, tiled=False)
+def exchange(value, axis, groups=None):
+    return lax.all_to_all(value, axis, 0, 0, tiled=False, axis_index_groups=groups)
 
 
 def shards(
@@ -295,7 +303,7 @@
         scratch=[*fetched(*picked), pltpu.SemaphoreType.DMA((3,))],
         limit=LARGE,
     )
-    arrived = exchange(outgoing, "hst")
+    arrived = exchange(outgoing, "hst", [[host_of(rank, FIRST) for rank in range(hosts)]])
     ordered = call(
         order_counts,
         shape((locals_, rows, length)),
@@ -309,7 +317,11 @@
         call(join_table, shape((locals_, rows, length + width)), arrived, ordered), "local"
     )
     pooled = call(pool, shape((length, width)), both.reshape(locals_ * rows, length + width))
-    moved = exchange(pooled.reshape(hosts, samples, width), "hst")
+    moved = exchange(
+        pooled.reshape(hosts, samples, width),
+        "hst",
+        [[host_of(rank, SECOND) for rank in range(hosts)]],
+    )
 
     made = (
         shape((state_rows, width)),

time: 107 us -> 101 us (0.944)
  waiting for transfers between devices: 6.71 us -> 0.01 us
  starting transfers between devices: 17.1 us -> 19 us
  blocking collectives: 71.2 us -> 69.4 us
    all_to_all x1, waiting for transfers between devices: 6.71 us -> 0.01 us  [exchange(): lax.all_to_all(value, axis, 0, 0, tiled=False, axis_index_groups=groups)]
    all_to_all x1, starting transfers between devices: 17.1 us -> 19 us  [exchange(): lax.all_to_all(value, axis, 0, 0, tiled=False, axis_index_groups=groups)]
    all_to_all x6, blocking collectives: 71.2 us -> 69.4 us  [exchange(): lax.all_to_all(value, axis, 0, 0, tiled=False, axis_index_groups=groups)]
  transfers between devices with their start and end apart: 1 -> 1, of which waited for: 1 -> 0; matrix products, arithmetic and copies ran while one was open for 0% -> 0% of each run, Pallas kernels for 2% -> 2%
where the time goes in v4:
time: 101 us; the launch traced here: 100 us
  blocking collectives  69.4 us (69%)
  starting transfers between devices  19 us (19%)
  Pallas kernels  9.75 us (10%)
  local copies, waits for them, and re-layouts  1.97 us (2%)
    all_to_all x6, blocking collectives, exchange(): lax.all_to_all(value, axis, 0, 0, tiled=False, axis_index_groups=groups)  69.4 us
    all_to_all x1, starting transfers between devices, exchange(): lax.all_to_all(value, axis, 0, 0, tiled=False, axis_index_groups=groups)  19 us
    pallas_call x9, Pallas kernels, call(): pl.pallas_call(kernel, out_shape=out_shape, in_specs=[pl.BlockSpec(memory...  9.75 us
  transfers between devices with their start and end apart: 1, of which 0 were waited for; matrix products, arithmetic and copies ran while one was open for 0% of the time, Pallas kernels for 2%

profile of v4, /device:TPU:1, one launch (start us, length us, event | category | flops | bytes accessed | tf_op | source)
XLA Modules:
  0.0 100.2 jit_solution(4150744780659020216)
XLA Ops:
  0.0 1.7 %shard_map.100 = f32[64,1,256]{2,1,0:T(1,128)} custom-call(s32[1,64]{1,0:T(1,128)} %bitcast.25, s32[1,64]{1,0:T(1,128)} %bitcast.30, bf16[64,256]{1,0:T(8,128)(2,1)} %bitcast.29), custom_call_target="tpu_custom_call" | custom-call | bytes 33280 | tf_op jit(solution)/shard_map/pallas_call | solution.py:251
  1.7 19.0 %all-to-all-start = ((f32[64,1,256]{2,1,0:T(1,128)}), f32[64,1,256]{2,1,0:T(1,128)S(1)}, u32[]{:S(2)}, u32[]{:S(2)}) async-start(f32[64,1,256]{2,1,0:T(1,128)} %shard_map.100), calls=%async_computation | async-start | bytes 131072 | tf_op jit(solution)/shard_map/all_to_all | solution.py:264
  20.8 0.0 copy-start.6
  20.8 1.2 %copy-done.6 = s32[1,4096,64]{1,2,0:T(8,128)S(1)} copy-done((s32[1,4096,64]{1,2,0:T(8,128)S(1)}, s32[1,4096,64]{1,2,0:T(8,128)}, u32[]{:S(2)}) %copy-start.6) | copy-done | bytes 1048600
  22.0 0.0 copy-start.7
  22.0 0.7 copy-done.7
  22.7 0.0 copy-start.2
  22.7 0.0 copy-start.3
  22.7 0.0 copy-start.5
  22.7 2.4 %shard_map.101.ordered_ref = bf16[8,64,512]{2,1,0:T(8,128)(2,1)S(1)} custom-call(s32[64,4096]{1,0:T(8,128)S(1)} %bitcast.27, s32[32,128]{1,0:T(8,128)S(1)} %bitcast.28), custom_call_target="tpu_custom_call" | custom-call | flops 603979776 | bytes 1064960 | tf_op jit(solution)/shard_map/pallas_call | solution.py:251
  25.2 0.0 all-to-all-done.arrived_ref
  25.2 0.2 shard_map.102
  25.4 17.5 %all_to_all.35 = bf16[8,64,768]{2,1,0:T(8,128)(2,1)S(1)} all-to-all(bf16[8,64,768]{2,1,0:T(8,128)(2,1)S(1)} %shard_map.102), channel_id=1, replica_groups=mesh['hst'=64,'local'=8] {'local'}, dimensions={0} | all-to-all | bytes 1572864 | tf_op jit(solution)/shard_map/all_to_all | solution.py:264
  42.9 0.3 shard_map.103
  43.2 0.0 copy-start.1
  43.3 0.0 copy-start.4
  43.3 17.6 %all_to_all.36 = bf16[64,8,256]{2,1,0:T(8,128)(2,1)S(1)} all-to-all(bf16[64,8,256]{2,1,0:T(8,128)(2,1)S(1)} %bitcast.18), channel_id=1, replica_groups={{288,296,304,312,256,264,272,280,352,360,368,376,320,328,336,344,416,42..., dimensions={0} | all-to-all | bytes 524288 | tf_op jit(solution)/shard_map/all_to_all | solution.py:264
  60.9 0.0 copy-done.2
  60.9 0.0 copy-done.3
  60.9 0.0 copy-done.5
  60.9 0.0 copy-start
  60.9 1.6 %shard_map.104 = (bf16[512,256]{1,0:T(8,128)(2,1)S(1)}, bf16[8,8,768]{2,1,0:T(8,128)(2,1)S(1)}, bf16[1,768,1024]{2,1,0:T(8,128)(2,1)S(1)}) custom-call(bf16[2,768,1024]{2,1,0:T(8,128)(2,1)} %refs_1_.1, bf16[512,256]{1,0:T(8,128)(2,1)S(1)} %bitcast.17, s32[1,64]{1,0:T(1,128)S(1)} %bitcast.26, bf16[12,2,64]{2,1,0:T(2,128)(2,1)S(1)} %bitcast.23, ...), custom_call_target="tpu_custom_call" | custom-call | bytes 3417344 | tf_op jit(solution)/shard_map/pallas_call | solution.py:251
  62.5 9.1 %all_to_all.37 = bf16[8,8,768]{2,1,0:T(8,128)(2,1)S(1)} all-to-all(bf16[8,8,768]{2,1,0:T(8,128)(2,1)S(1)} %get-tuple-element.10), channel_id=1, replica_groups=mesh['hst'=64,'local'=8] {'local'}, dimensions={0} | all-to-all | bytes 196608 | tf_op jit(solution)/shard_map/all_to_all | solution.py:264
  71.6 0.7 shard_map.105
  72.3 8.5 %all_to_all.38.refs_0_ = bf16[8,8,1024]{2,1,0:T(8,128)(2,1)S(1)} all-to-all(bf16[8,8,1024]{2,1,0:T(8,128)(2,1)S(1)} %bitcast.19), channel_id=1, replica_groups=mesh['hst'=64,'local'=8] {'local'}, dimensions={0} | all-to-all | bytes 262144 | tf_op jit(solution)/shard_map/all_to_all | solution.py:264
  80.7 0.0 copy-done.1
  80.7 0.0 copy-done.4
  80.7 1.0 shard_map.106
  81.7 8.2 %all_to_all.39 = bf16[8,8,768]{2,1,0:T(8,128)(2,1)S(1)} all-to-all(bf16[8,8,768]{2,1,0:T(8,128)(2,1)S(1)} %get-tuple-element.13), channel_id=1, replica_groups=mesh['hst'=64,'local'=8] {'local'}, dimensions={0} | all-to-all | bytes 196608 | tf_op jit(solution)/shard_map/all_to_all | solution.py:264
  90.0 0.0 copy-done
  90.0 0.7 shard_map.107
  90.7 8.5 %all_to_all.40.refs_0_ = bf16[8,8,1024]{2,1,0:T(8,128)(2,1)S(1)} all-to-all(bf16[8,8,1024]{2,1,0:T(8,128)(2,1)S(1)} %bitcast.20), channel_id=1, replica_groups=mesh['hst'=64,'local'=8] {'local'}, dimensions={0} | all-to-all | bytes 262144 | tf_op jit(solution)/shard_map/all_to_all | solution.py:264
  99.1 1.1 %shard_map.108 = bf16[512,256]{1,0:T(8,128)(2,1)} custom-call(bf16[8,8,1024]{2,1,0:T(8,128)(2,1)S(1)} %all_to_all.40.refs_0_, bf16[512,256]{1,0:T(8,128)(2,1)S(1)} %get-tuple-element.14.refs_1_, bf16[2,32,64]{2,1,0:T(8,128)(2,1)S(1)} %copy-done.1, f32[2,256]{1,0:T(2,128)S(1)} %copy-done.4), custom_call_target="tpu_custom_call" | custom-call | bytes 403456 | tf_op jit(solution)/shard_map/pallas_call | solution.py:251
Async XLA Ops:
  1.7 23.4 %all-to-all-start = ((f32[64,1,256]{2,1,0:T(1,128)}), f32[64,1,256]{2,1,0:T(1,128)S(1)}, u32[]{:S(2)}, u32[]{:S(2)}) async-start(f32[64,1,256]{2,1,0:T(1,128)} %shard_map.100), calls=%async_computation | async-start | bytes 131072 | tf_op jit(solution)/shard_map/all_to_all | solution.py:264
  20.8 1.2 %copy-start.6 = (s32[1,4096,64]{1,2,0:T(8,128)S(1)}, s32[1,4096,64]{1,2,0:T(8,128)}, u32[]{:S(2)}) copy-start(s32[1,4096,64]{1,2,0:T(8,128)} %param.11) | copy-start | bytes 3145732
  22.0 0.7 copy-start.7
  22.7 38.1 %copy-start.2 = (bf16[2,64,12]{1,0,2:T(2,128)(2,1)S(1)}, bf16[2,64,12]{1,0,2:T(2,128)(2,1)}, u32[]{:S(2)}) copy-start(bf16[2,64,12]{1,0,2:T(2,128)(2,1)} %param.15) | copy-start | bytes 9220
  22.7 38.1 %copy-start.3 = (f32[2,768]{1,0:T(2,128)S(1)}, f32[2,768]{1,0:T(2,128)}, u32[]{:S(2)}) copy-start(f32[2,768]{1,0:T(2,128)} %refs_5_.1) | copy-start | bytes 18436
  22.7 38.1 %copy-start.5 = (s32[64]{0:T(128)S(1)}, s32[64]{0:T(128)}, u32[]{:S(2)}) copy-start(s32[64]{0:T(128)} %param.12) | copy-start | bytes 772
  43.2 37.5 %copy-start.1 = (bf16[2,32,64]{2,1,0:T(8,128)(2,1)S(1)}, bf16[2,32,64]{2,1,0:T(8,128)(2,1)}, u32[]{:S(2)}) copy-start(bf16[2,32,64]{2,1,0:T(8,128)(2,1)} %refs_2_.3) | copy-start | bytes 24580
  43.3 37.5 %copy-start.4 = (f32[2,256]{1,0:T(2,128)S(1)}, f32[2,256]{1,0:T(2,128)}, u32[]{:S(2)}) copy-start(f32[2,256]{1,0:T(2,128)} %refs_3_.3) | copy-start | bytes 6148
  60.9 29.1 %copy-start = (bf16[2,768,1024]{2,1,0:T(8,128)(2,1)S(1)}, bf16[2,768,1024]{2,1,0:T(8,128)(2,1)}, u32[]{:S(2)}) copy-start(bf16[2,768,1024]{2,1,0:T(8,128)(2,1)} %refs_1_.1) | copy-start | bytes 9437188

commit v5 on v4

--- a/solution.py
+++ b/solution.py
@@ -9,6 +9,7 @@
 PACK = 4
 LOW = 256
 LANES = 128
+NEAR, LAST = 5, 5
 SIDE = 8
 FIRST, SECOND = (6, 4), (4, 4)
 SMALL, MIDDLE, LARGE = 40 << 20, 49 << 20, 60 << 20
@@ -41,6 +42,10 @@
     for copy in copies:
         copy.start()
     return copies
+
+
+def local_of(rank, start):
+    return (rank + start) % 8
 
 
 def host_of(rank, start):
@@ -73,11 +78,9 @@
     order = order_ref[...]
     parts = jnp.concatenate([order >> 8, order & (LOW - 1)], axis=0).astype(F32).astype(BF16)
     for target in range(targets):
-        m = number((LANES, length), 1)
-        row = host_of(m // samples, SECOND) * (targets * samples) + target * samples + m % samples
+        m = number((1, length), 1)
+        row = host_of(m // samples, SECOND) * (targets * samples) + local_of(target, NEAR) * samples + m % samples
         found = matmul(parts, ones_where(number((LANES, length), 0) == row % LANES))
-        m = number((2 * order_rows, length), 1)
-        row = host_of(m // samples, SECOND) * (targets * samples) + target * samples + m % samples
         found = jnp.where(
             number((2 * order_rows, length), 0) % order_rows == row // LANES, found, 0.0
         )
@@ -213,7 +216,7 @@
     tables = rows // samples
     mixed = jnp.concatenate(
         [
-            mixed_ref[source, :, start : start + width].astype(F32)
+            mixed_ref[(source - LAST) % sources, :, start : start + width].astype(F32)
             for source in range(sources)
             for start in range(0, part, width)
         ],
@@ -314,7 +317,9 @@
         flops=2 * batch * (LOW * LOW + 64 * LANES),
     )
     both = exchange(
-        call(join_table, shape((locals_, rows, length + width)), arrived, ordered), "local"
+        call(join_table, shape((locals_, rows, length + width)), arrived, ordered),
+        "local",
+        [[local_of(rank, NEAR) for rank in range(locals_)]],
     )
     pooled = call(pool, shape((length, width)), both.reshape(locals_ * rows, length + width))
     moved = exchange(
@@ -339,15 +344,16 @@
         scratch=[pltpu.SemaphoreType.DMA((1,))],
         limit=MIDDLE,
     )
+    last = [[local_of(rank, LAST) for rank in range(locals_)]]
     for layer in range(LAYERS):
-        gathered = exchange(flat, "local").reshape(locals_ * samples, flat_size)
+        gathered = exchange(flat, "local", last).reshape(locals_ * samples, flat_size)
         columns = call(
             lambda *refs, layer=layer: map_columns(layer, rank, *refs),
             shape((locals_ * samples, fm_weight.shape[2])),
             gathered,
             fm_weight if layer else weight,
         )
-        mixed = exchange(columns.reshape(locals_, samples, -1), "local")
+        mixed = exchange(columns.reshape(locals_, samples, -1), "local", last)
         if layer + 1 < LAYERS:
             state, flat = call(
                 lambda *refs, layer=layer: next_layer(layer, *refs),

time: 101 us -> 95.8 us (0.949)
  blocking collectives: 69.4 us -> 64.4 us
    all_to_all x6, blocking collectives: 69.4 us -> 64.4 us  [exchange(): lax.all_to_all(value, axis, 0, 0, tiled=False, axis_index_groups=groups)]
  transfers between devices with their start and end apart: 1 -> 1, of which waited for: 0 -> 0; matrix products, arithmetic and copies ran while one was open for 0% -> 0% of each run, Pallas kernels for 2% -> 3%
where the time goes in v5:
time: 95.8 us; the launch traced here: 95.3 us
  blocking collectives  64.4 us (67%)
  starting transfers between devices  19 us (20%)
  Pallas kernels  9.75 us (10%)
  local copies, waits for them, and re-layouts  1.97 us (2%)
    all_to_all x6, blocking collectives, exchange(): lax.all_to_all(value, axis, 0, 0, tiled=False, axis_index_groups=groups)  64.4 us
    all_to_all x1, starting transfers between devices, exchange(): lax.all_to_all(value, axis, 0, 0, tiled=False, axis_index_groups=groups)  19 us
    pallas_call x9, Pallas kernels, call(): pl.pallas_call(kernel, out_shape=out_shape, in_specs=[pl.BlockSpec(memory...  9.75 us
    unnamed x16, local copies, waits for them, and re-layouts  1.97 us
  transfers between devices with their start and end apart: 1, of which 0 were waited for; matrix products, arithmetic and copies ran while one was open for 0% of the time, Pallas kernels for 3%

profile of v5, /device:TPU:1, one launch (start us, length us, event | category | flops | bytes accessed | tf_op | source)
XLA Modules:
  0.0 95.3 jit_solution(6327212281161086473)
XLA Ops:
  0.0 1.7 %shard_map.100 = f32[64,1,256]{2,1,0:T(1,128)} custom-call(s32[1,64]{1,0:T(1,128)} %bitcast.25, s32[1,64]{1,0:T(1,128)} %bitcast.30, bf16[64,256]{1,0:T(8,128)(2,1)} %bitcast.29), custom_call_target="tpu_custom_call" | custom-call | bytes 33280 | tf_op jit(solution)/shard_map/pallas_call | solution.py:254
  1.7 19.0 %all-to-all-start = ((f32[64,1,256]{2,1,0:T(1,128)}), f32[64,1,256]{2,1,0:T(1,128)S(1)}, u32[]{:S(2)}, u32[]{:S(2)}) async-start(f32[64,1,256]{2,1,0:T(1,128)} %shard_map.100), calls=%async_computation | async-start | bytes 131072 | tf_op jit(solution)/shard_map/all_to_all | solution.py:267
  20.8 0.0 copy-start.6
  20.8 1.2 %copy-done.6 = s32[1,4096,64]{1,2,0:T(8,128)S(1)} copy-done((s32[1,4096,64]{1,2,0:T(8,128)S(1)}, s32[1,4096,64]{1,2,0:T(8,128)}, u32[]{:S(2)}) %copy-start.6) | copy-done | bytes 1048600
  22.0 0.0 copy-start.7
  22.0 0.7 copy-done.7
  22.7 0.0 copy-start.2
  22.7 0.0 copy-start.3
  22.7 0.0 copy-start.5
  22.7 2.4 %shard_map.101.ordered_ref = bf16[8,64,512]{2,1,0:T(8,128)(2,1)S(1)} custom-call(s32[64,4096]{1,0:T(8,128)S(1)} %bitcast.27, s32[32,128]{1,0:T(8,128)S(1)} %bitcast.28), custom_call_target="tpu_custom_call" | custom-call | flops 603979776 | bytes 1064960 | tf_op jit(solution)/shard_map/pallas_call | solution.py:254
  25.2 0.0 all-to-all-done.arrived_ref
  25.2 0.2 shard_map.102
  25.4 15.0 %all_to_all.35 = bf16[8,64,768]{2,1,0:T(8,128)(2,1)S(1)} all-to-all(bf16[8,64,768]{2,1,0:T(8,128)(2,1)S(1)} %shard_map.102), channel_id=1, replica_groups={{5,6,7,0,1,2,3,4},{13,14,15,8,9,10,11,12},{21,22,23,16,17,18,19,20},{29..., dimensions={0} | all-to-all | bytes 1572864 | tf_op jit(solution)/shard_map/all_to_all | solution.py:267
  40.4 0.3 shard_map.103
  40.8 0.0 copy-start.1
  40.8 0.0 copy-start.4
  40.8 17.6 %all_to_all.36 = bf16[64,8,256]{2,1,0:T(8,128)(2,1)S(1)} all-to-all(bf16[64,8,256]{2,1,0:T(8,128)(2,1)S(1)} %bitcast.18), channel_id=1, replica_groups={{288,296,304,312,256,264,272,280,352,360,368,376,320,328,336,344,416,42..., dimensions={0} | all-to-all | bytes 524288 | tf_op jit(solution)/shard_map/all_to_all | solution.py:267
  58.4 0.0 copy-done.2
  58.4 0.0 copy-done.3
  58.4 0.0 copy-done.5
  58.4 0.0 copy-start
  58.4 1.6 %shard_map.104 = (bf16[512,256]{1,0:T(8,128)(2,1)S(1)}, bf16[8,8,768]{2,1,0:T(8,128)(2,1)S(1)}, bf16[1,768,1024]{2,1,0:T(8,128)(2,1)S(1)}) custom-call(bf16[2,768,1024]{2,1,0:T(8,128)(2,1)} %refs_1_.1, bf16[512,256]{1,0:T(8,128)(2,1)S(1)} %bitcast.17, s32[1,64]{1,0:T(1,128)S(1)} %bitcast.26, bf16[12,2,64]{2,1,0:T(2,128)(2,1)S(1)} %bitcast.23, ...), custom_call_target="tpu_custom_call" | custom-call | bytes 3417344 | tf_op jit(solution)/shard_map/pallas_call | solution.py:254
  60.0 8.9 %all_to_all.37 = bf16[8,8,768]{2,1,0:T(8,128)(2,1)S(1)} all-to-all(bf16[8,8,768]{2,1,0:T(8,128)(2,1)S(1)} %get-tuple-element.10), channel_id=1, replica_groups={{5,6,7,0,1,2,3,4},{13,14,15,8,9,10,11,12},{21,22,23,16,17,18,19,20},{29..., dimensions={0} | all-to-all | bytes 196608 | tf_op jit(solution)/shard_map/all_to_all | solution.py:267
  68.9 0.7 shard_map.105
  69.6 7.4 %all_to_all.38.refs_0_ = bf16[8,8,1024]{2,1,0:T(8,128)(2,1)S(1)} all-to-all(bf16[8,8,1024]{2,1,0:T(8,128)(2,1)S(1)} %bitcast.19), channel_id=1, replica_groups={{5,6,7,0,1,2,3,4},{13,14,15,8,9,10,11,12},{21,22,23,16,17,18,19,20},{29..., dimensions={0} | all-to-all | bytes 262144 | tf_op jit(solution)/shard_map/all_to_all | solution.py:267
  77.1 0.0 copy-done.1
  77.1 0.0 copy-done.4
  77.1 1.0 %shard_map.106 = (bf16[512,256]{1,0:T(8,128)(2,1)S(1)}, bf16[8,8,768]{2,1,0:T(8,128)(2,1)S(1)}) custom-call(bf16[8,8,1024]{2,1,0:T(8,128)(2,1)S(1)} %all_to_all.38.refs_0_, bf16[512,256]{1,0:T(8,128)(2,1)S(1)} %get-tuple-element.12.refs_1_, bf16[2,32,64]{2,1,0:T(8,128)(2,1)S(1)} %copy-done.1, f32[2,256]{1,0:T(2,128)S(1)} %copy-done.4, ...), custom_call_target="tpu_custom_call" | custom-call | bytes 412672 | tf_op jit(solution)/shard_map/pallas_call | solution.py:254
  78.1 7.7 %all_to_all.39 = bf16[8,8,768]{2,1,0:T(8,128)(2,1)S(1)} all-to-all(bf16[8,8,768]{2,1,0:T(8,128)(2,1)S(1)} %get-tuple-element.13), channel_id=1, replica_groups={{5,6,7,0,1,2,3,4},{13,14,15,8,9,10,11,12},{21,22,23,16,17,18,19,20},{29..., dimensions={0} | all-to-all | bytes 196608 | tf_op jit(solution)/shard_map/all_to_all | solution.py:267
  85.8 0.0 copy-done
  85.8 0.7 shard_map.107
  86.5 7.7 %all_to_all.40.refs_0_ = bf16[8,8,1024]{2,1,0:T(8,128)(2,1)S(1)} all-to-all(bf16[8,8,1024]{2,1,0:T(8,128)(2,1)S(1)} %bitcast.20), channel_id=1, replica_groups={{5,6,7,0,1,2,3,4},{13,14,15,8,9,10,11,12},{21,22,23,16,17,18,19,20},{29..., dimensions={0} | all-to-all | bytes 262144 | tf_op jit(solution)/shard_map/all_to_all | solution.py:267
  94.2 1.1 %shard_map.108 = bf16[512,256]{1,0:T(8,128)(2,1)} custom-call(bf16[8,8,1024]{2,1,0:T(8,128)(2,1)S(1)} %all_to_all.40.refs_0_, bf16[512,256]{1,0:T(8,128)(2,1)S(1)} %get-tuple-element.14.refs_1_, bf16[2,32,64]{2,1,0:T(8,128)(2,1)S(1)} %copy-done.1, f32[2,256]{1,0:T(2,128)S(1)} %copy-done.4), custom_call_target="tpu_custom_call" | custom-call | bytes 403456 | tf_op jit(solution)/shard_map/pallas_call | solution.py:254
Async XLA Ops:
  1.7 23.4 %all-to-all-start = ((f32[64,1,256]{2,1,0:T(1,128)}), f32[64,1,256]{2,1,0:T(1,128)S(1)}, u32[]{:S(2)}, u32[]{:S(2)}) async-start(f32[64,1,256]{2,1,0:T(1,128)} %shard_map.100), calls=%async_computation | async-start | bytes 131072 | tf_op jit(solution)/shard_map/all_to_all | solution.py:267
  20.8 1.2 %copy-start.6 = (s32[1,4096,64]{1,2,0:T(8,128)S(1)}, s32[1,4096,64]{1,2,0:T(8,128)}, u32[]{:S(2)}) copy-start(s32[1,4096,64]{1,2,0:T(8,128)} %param.11) | copy-start | bytes 3145732
  22.0 0.7 copy-start.7
  22.7 35.7 %copy-start.2 = (bf16[2,64,12]{1,0,2:T(2,128)(2,1)S(1)}, bf16[2,64,12]{1,0,2:T(2,128)(2,1)}, u32[]{:S(2)}) copy-start(bf16[2,64,12]{1,0,2:T(2,128)(2,1)} %param.15) | copy-start | bytes 9220
  22.7 35.7 %copy-start.3 = (f32[2,768]{1,0:T(2,128)S(1)}, f32[2,768]{1,0:T(2,128)}, u32[]{:S(2)}) copy-start(f32[2,768]{1,0:T(2,128)} %refs_5_.1) | copy-start | bytes 18436
  22.7 35.7 %copy-start.5 = (s32[64]{0:T(128)S(1)}, s32[64]{0:T(128)}, u32[]{:S(2)}) copy-start(s32[64]{0:T(128)} %param.12) | copy-start | bytes 772
  40.8 36.3 %copy-start.1 = (bf16[2,32,64]{2,1,0:T(8,128)(2,1)S(1)}, bf16[2,32,64]{2,1,0:T(8,128)(2,1)}, u32[]{:S(2)}) copy-start(bf16[2,32,64]{2,1,0:T(8,128)(2,1)} %refs_2_.3) | copy-start | bytes 24580
  40.8 36.3 %copy-start.4 = (f32[2,256]{1,0:T(2,128)S(1)}, f32[2,256]{1,0:T(2,128)}, u32[]{:S(2)}) copy-start(f32[2,256]{1,0:T(2,128)} %refs_3_.3) | copy-start | bytes 6148
  58.4 27.4 %copy-start = (bf16[2,768,1024]{2,1,0:T(8,128)(2,1)S(1)}, bf16[2,768,1024]{2,1,0:T(8,128)(2,1)}, u32[]{:S(2)}) copy-start(bf16[2,768,1024]{2,1,0:T(8,128)(2,1)} %refs_1_.1) | copy-start | bytes 9437188

commit v6 on v5

--- a/solution.py
+++ b/solution.py
@@ -12,7 +12,7 @@
 NEAR, LAST = 5, 5
 SIDE = 8
 FIRST, SECOND = (6, 4), (4, 4)
-SMALL, MIDDLE, LARGE = 40 << 20, 49 << 20, 60 << 20
+SMALL, MIDDLE, MORE, LARGE = 40 << 20, 49 << 20, 53 << 20, 60 << 20
 F32 = jnp.float32
 BF16 = jnp.bfloat16
 
@@ -62,30 +62,36 @@
     out_ref[:, 0, :] = matmul(chosen, stored_ref[...])
 
 
-def order_counts(counts_ref, order_ref, out_ref, packed_ref):
+def order_counts(counts_hbm, order_ref, out_ref, packed_ref, counts_ref, sems):
+    copies = fetch([(counts_hbm, counts_ref)], sems)
     rows, batch = counts_ref.shape
     targets, _, length = out_ref.shape
     words = rows // PACK
     high_count = batch // LOW
     order_rows = order_ref.shape[0]
     samples = 8
+    order = order_ref[...]
+    parts = jnp.concatenate([order >> 8, order & (LOW - 1)], axis=0).astype(F32).astype(BF16)
+    places = []
+    for target in range(targets):
+        m = number((1, length), 1)
+        row = host_of(m // samples, SECOND) * (targets * samples)
+        row = row + local_of(target, NEAR) * samples + m % samples
+        found = matmul(parts, ones_where(number((LANES, length), 0) == row % LANES))
+        found = jnp.where(
+            number((2 * order_rows, length), 0) % order_rows == row // LANES, found, 0.0
+        )
+        high_part = jnp.sum(found[:order_rows], axis=0, keepdims=True).astype(jnp.int32)
+        low_part = jnp.sum(found[order_rows:], axis=0, keepdims=True).astype(jnp.int32)
+        places.append((high_part, low_part))
+    copies[0].wait()
     word = counts_ref[0:words, :]
     for k in range(1, PACK):
         word = word + (counts_ref[k * words : (k + 1) * words, :] << (2 * k))
     word = word.astype(F32).astype(BF16)
     for high in range(high_count):
         packed_ref[high * words : (high + 1) * words, :] = word[:, high * LOW : (high + 1) * LOW]
-    order = order_ref[...]
-    parts = jnp.concatenate([order >> 8, order & (LOW - 1)], axis=0).astype(F32).astype(BF16)
-    for target in range(targets):
-        m = number((1, length), 1)
-        row = host_of(m // samples, SECOND) * (targets * samples) + local_of(target, NEAR) * samples + m % samples
-        found = matmul(parts, ones_where(number((LANES, length), 0) == row % LANES))
-        found = jnp.where(
-            number((2 * order_rows, length), 0) % order_rows == row // LANES, found, 0.0
-        )
-        high_part = jnp.sum(found[:order_rows], axis=0, keepdims=True).astype(jnp.int32)
-        low_part = jnp.sum(found[order_rows:], axis=0, keepdims=True).astype(jnp.int32)
+    for target, (high_part, low_part) in enumerate(places):
         picked = matmul(packed_ref[...], ones_where(number((LOW, length), 0) == low_part))
         value = jnp.zeros((words, length), F32)
         for high in range(high_count):
@@ -118,9 +124,9 @@
     few, tables = matrix.shape
     rows, columns = few * samples, samples * tables
     tall = ones_where(number((rows, few), 0) // samples == number((rows, few), 1))
-    wide = ones_where(number((tables, columns), 1) % tables == number((tables, columns), 0))
+    wide = ones_where(number((1, columns), 1) % tables == number((tables, columns), 0))
     values = matmul(matmul(tall, matrix).astype(BF16), wide)
-    own = number((rows, columns), 0) % samples == number((rows, columns), 1) // tables
+    own = number((rows, columns), 0) % samples == number((1, columns), 1) // tables
     return jnp.where(own, values, 0.0).astype(BF16)
 
 
@@ -134,11 +140,10 @@
 def gain_blocks(gain, rank):
     flat = gain.shape[1]
     tables = flat // rank
-    lane = number((16, flat), 1)
-    own = lane % rank == number((16, flat), 0)
-    to_table = ones_where(
-        number((flat, LANES), 0) // rank == number((flat, LANES), 1) % tables
-    )
+    own = number((1, flat), 1) % rank == number((16, flat), 0)
+    row = number((flat, LANES), 0)
+    least = number((1, LANES), 1) % tables * rank
+    to_table = ones_where((row >= least) & (row < least + rank))
     total = jnp.zeros((16, LANES), F32)
     for _ in range(3):
         part = gain.astype(BF16).astype(F32)
@@ -161,7 +166,7 @@
     gain = jnp.concatenate(gain_blocks(gain_ref[layer : layer + 1, :], rank), axis=1)
     inner = matmul(proj, state).astype(BF16)
     inter = matmul_nt(inner, state)
-    own = number(inter.shape, 0) % samples == number(inter.shape, 1) // tables
+    own = number(inter.shape, 0) % samples == number((1, rows), 1) // tables
     inter = jnp.where(own, inter, 0.0)
     while inter.shape[1] > LANES:
         half = inter.shape[1] // 2
@@ -189,9 +194,9 @@
     samples = rows // tables
     holder = ones_where(host_of(number((tables, tables), 0), SECOND) == host_ref[...])
     tall = ones_where(number((rows, tables), 0) % tables == number((rows, tables), 1))
-    wide = ones_where(number((tables, rows), 1) // samples == number((tables, rows), 0))
+    wide = ones_where(number((1, rows), 1) // samples == number((tables, rows), 0))
     place = matmul(matmul_nt(tall, holder).astype(BF16), wide)
-    own = number((rows, rows), 0) // tables == number((rows, rows), 1) % samples
+    own = number((rows, rows), 0) // tables == number((1, rows), 1) % samples
     place = jnp.where(own, place, 0.0).astype(BF16)
     state = matmul(place, moved_ref[...]).astype(BF16)
     state_ref[...] = state
@@ -202,8 +207,10 @@
 def map_columns(layer, rank, flat_ref, weight_ref, out_ref):
     flat = flat_ref.shape[1]
     tables = flat // rank
-    row = number((flat, flat), 0)
-    order = ones_where((row % tables) * rank + row // tables == number((flat, flat), 1))
+    column = number((1, flat), 1)
+    order = ones_where(
+        number((flat, flat), 0) == (column % rank) * tables + column // rank
+    )
     out_ref[...] = matmul(
         matmul(flat_ref[...], order).astype(BF16), weight_ref[min(layer, weight_ref.shape[0] - 1)]
     ).astype(BF16)
@@ -222,9 +229,10 @@
         ],
         axis=0,
     ).astype(BF16)
-    row = number((made * samples, made * samples), 0)
+    column = number((1, made * samples), 1)
     turn = ones_where(
-        (row % made) * samples + row // made == number((made * samples, made * samples), 1)
+        number((made * samples, made * samples), 0)
+        == (column % samples) * made + column // samples
     )
     mixed = matmul(turn, mixed)
     joined = []
@@ -307,14 +315,19 @@
         limit=LARGE,
     )
     arrived = exchange(outgoing, "hst", [[host_of(rank, FIRST) for rank in range(hosts)]])
+    by_row = jnp.transpose(counts[0])
     ordered = call(
         order_counts,
         shape((locals_, rows, length)),
-        jnp.transpose(counts[0]),
         owner_order.reshape(batch // LANES, LANES),
-
-        scratch=[pltpu.VMEM((batch // LOW * (rows // PACK), LOW), BF16)],
+        own=(by_row,),
+        scratch=[
+            pltpu.VMEM((batch // LOW * (rows // PACK), LOW), BF16),
+            *fetched(by_row),
+            pltpu.SemaphoreType.DMA((1,)),
+        ],
         flops=2 * batch * (LOW * LOW + 64 * LANES),
+        limit=MORE,
     )
     both = exchange(
         call(join_table, shape((locals_, rows, length + width)), arrived, ordered),

time: 95.8 us -> 95.7 us (level)
  local copies, waits for them, and re-layouts: 1.97 us -> 0.74 us
    unnamed x16 -> x14, local copies, waits for them, and re-layouts: 1.97 us -> 0.74 us
  transfers between devices with their start and end apart: 1 -> 1, of which waited for: 0 -> 1; matrix products, arithmetic and copies ran while one was open for 0% -> 0% of each run, Pallas kernels for 3% -> 3%
where the time goes in v6:
time: 95.7 us; the launch traced here: 95.2 us
  blocking collectives  64.7 us (68%)
  starting transfers between devices  19 us (20%)
  Pallas kernels  9.65 us (10%)
    all_to_all x6, blocking collectives, exchange(): lax.all_to_all(value, axis, 0, 0, tiled=False, axis_index_groups=groups)  64.7 us
    all_to_all x1, starting transfers between devices, exchange(): lax.all_to_all(value, axis, 0, 0, tiled=False, axis_index_groups=groups)  19 us
    pallas_call x9, Pallas kernels, call(): pl.pallas_call(kernel, out_shape=out_shape, in_specs=[pl.BlockSpec(memory...  9.65 us
  transfers between devices with their start and end apart: 1, of which 1 were waited for; matrix products, arithmetic and copies ran while one was open for 0% of the time, Pallas kernels for 3%

profile of v6, /device:TPU:1, one launch (start us, length us, event | category | flops | bytes accessed | tf_op | source)
XLA Modules:
  0.0 95.2 jit_solution(17281153761578741935)
XLA Ops:
  0.0 1.7 %shard_map.100 = f32[64,1,256]{2,1,0:T(1,128)} custom-call(s32[1,64]{1,0:T(1,128)} %bitcast.25, s32[1,64]{1,0:T(1,128)} %bitcast.29, bf16[64,256]{1,0:T(8,128)(2,1)} %bitcast.28), custom_call_target="tpu_custom_call" | custom-call | bytes 33280 | tf_op jit(solution)/shard_map/pallas_call | solution.py:262
  1.7 19.0 %all-to-all-start = ((f32[64,1,256]{2,1,0:T(1,128)}), f32[64,1,256]{2,1,0:T(1,128)S(1)}, u32[]{:S(2)}, u32[]{:S(2)}) async-start(f32[64,1,256]{2,1,0:T(1,128)} %shard_map.100), calls=%async_computation | async-start | bytes 131072 | tf_op jit(solution)/shard_map/all_to_all | solution.py:275
  20.8 0.0 copy-start.6
  20.8 0.7 copy-done.6
  21.5 0.0 copy-start.2
  21.5 0.0 copy-start.3
  21.5 0.0 copy-start.5
  21.5 2.4 %shard_map.101.ordered_ref = bf16[8,64,512]{2,1,0:T(8,128)(2,1)S(1)} custom-call(s32[64,4096]{1,0:T(8,128)} %bitcast.30, s32[32,128]{1,0:T(8,128)S(1)} %bitcast.27), custom_call_target="tpu_custom_call" | custom-call | flops 603979776 | bytes 1064960 | tf_op jit(solution)/shard_map/pallas_call | solution.py:262
  23.9 0.9 all-to-all-done.arrived_ref
  24.8 0.2 shard_map.102
  25.1 15.4 %all_to_all.35 = bf16[8,64,768]{2,1,0:T(8,128)(2,1)S(1)} all-to-all(bf16[8,64,768]{2,1,0:T(8,128)(2,1)S(1)} %shard_map.102), channel_id=1, replica_groups={{5,6,7,0,1,2,3,4},{13,14,15,8,9,10,11,12},{21,22,23,16,17,18,19,20},{29..., dimensions={0} | all-to-all | bytes 1572864 | tf_op jit(solution)/shard_map/all_to_all | solution.py:275
  40.4 0.3 shard_map.103
  40.8 0.0 copy-start.1
  40.8 0.0 copy-start.4
  40.8 17.6 %all_to_all.36 = bf16[64,8,256]{2,1,0:T(8,128)(2,1)S(1)} all-to-all(bf16[64,8,256]{2,1,0:T(8,128)(2,1)S(1)} %bitcast.18), channel_id=1, replica_groups={{288,296,304,312,256,264,272,280,352,360,368,376,320,328,336,344,416,42..., dimensions={0} | all-to-all | bytes 524288 | tf_op jit(solution)/shard_map/all_to_all | solution.py:275
  58.4 0.0 copy-done.2
  58.4 0.0 copy-done.3
  58.4 0.0 copy-done.5
  58.4 0.0 copy-start
  58.4 1.6 %shard_map.104 = (bf16[512,256]{1,0:T(8,128)(2,1)S(1)}, bf16[8,8,768]{2,1,0:T(8,128)(2,1)S(1)}, bf16[1,768,1024]{2,1,0:T(8,128)(2,1)S(1)}) custom-call(bf16[2,768,1024]{2,1,0:T(8,128)(2,1)} %refs_1_.1, bf16[512,256]{1,0:T(8,128)(2,1)S(1)} %bitcast.17, s32[1,64]{1,0:T(1,128)S(1)} %bitcast.26, bf16[12,2,64]{2,1,0:T(2,128)(2,1)S(1)} %bitcast.23, ...), custom_call_target="tpu_custom_call" | custom-call | bytes 3417344 | tf_op jit(solution)/shard_map/pallas_call | solution.py:262
  60.0 8.9 %all_to_all.37 = bf16[8,8,768]{2,1,0:T(8,128)(2,1)S(1)} all-to-all(bf16[8,8,768]{2,1,0:T(8,128)(2,1)S(1)} %get-tuple-element.10), channel_id=1, replica_groups={{5,6,7,0,1,2,3,4},{13,14,15,8,9,10,11,12},{21,22,23,16,17,18,19,20},{29..., dimensions={0} | all-to-all | bytes 196608 | tf_op jit(solution)/shard_map/all_to_all | solution.py:275
  68.9 0.6 shard_map.105
  69.6 7.4 %all_to_all.38.refs_0_ = bf16[8,8,1024]{2,1,0:T(8,128)(2,1)S(1)} all-to-all(bf16[8,8,1024]{2,1,0:T(8,128)(2,1)S(1)} %bitcast.19), channel_id=1, replica_groups={{5,6,7,0,1,2,3,4},{13,14,15,8,9,10,11,12},{21,22,23,16,17,18,19,20},{29..., dimensions={0} | all-to-all | bytes 262144 | tf_op jit(solution)/shard_map/all_to_all | solution.py:275
  77.0 0.0 copy-done.1
  77.0 0.0 copy-done.4
  77.0 1.0 %shard_map.106 = (bf16[512,256]{1,0:T(8,128)(2,1)S(1)}, bf16[8,8,768]{2,1,0:T(8,128)(2,1)S(1)}) custom-call(bf16[8,8,1024]{2,1,0:T(8,128)(2,1)S(1)} %all_to_all.38.refs_0_, bf16[512,256]{1,0:T(8,128)(2,1)S(1)} %get-tuple-element.12.refs_1_, bf16[2,32,64]{2,1,0:T(8,128)(2,1)S(1)} %copy-done.1, f32[2,256]{1,0:T(2,128)S(1)} %copy-done.4, ...), custom_call_target="tpu_custom_call" | custom-call | bytes 412672 | tf_op jit(solution)/shard_map/pallas_call | solution.py:262
  78.0 7.7 %all_to_all.39 = bf16[8,8,768]{2,1,0:T(8,128)(2,1)S(1)} all-to-all(bf16[8,8,768]{2,1,0:T(8,128)(2,1)S(1)} %get-tuple-element.13), channel_id=1, replica_groups={{5,6,7,0,1,2,3,4},{13,14,15,8,9,10,11,12},{21,22,23,16,17,18,19,20},{29..., dimensions={0} | all-to-all | bytes 196608 | tf_op jit(solution)/shard_map/all_to_all | solution.py:275
  85.7 0.0 copy-done
  85.7 0.6 shard_map.107
  86.4 7.7 %all_to_all.40.refs_0_ = bf16[8,8,1024]{2,1,0:T(8,128)(2,1)S(1)} all-to-all(bf16[8,8,1024]{2,1,0:T(8,128)(2,1)S(1)} %bitcast.20), channel_id=1, replica_groups={{5,6,7,0,1,2,3,4},{13,14,15,8,9,10,11,12},{21,22,23,16,17,18,19,20},{29..., dimensions={0} | all-to-all | bytes 262144 | tf_op jit(solution)/shard_map/all_to_all | solution.py:275
  94.1 1.1 %shard_map.108 = bf16[512,256]{1,0:T(8,128)(2,1)} custom-call(bf16[8,8,1024]{2,1,0:T(8,128)(2,1)S(1)} %all_to_all.40.refs_0_, bf16[512,256]{1,0:T(8,128)(2,1)S(1)} %get-tuple-element.14.refs_1_, bf16[2,32,64]{2,1,0:T(8,128)(2,1)S(1)} %copy-done.1, f32[2,256]{1,0:T(2,128)S(1)} %copy-done.4), custom_call_target="tpu_custom_call" | custom-call | bytes 403456 | tf_op jit(solution)/shard_map/pallas_call | solution.py:262
Async XLA Ops:
  1.7 23.1 %all-to-all-start = ((f32[64,1,256]{2,1,0:T(1,128)}), f32[64,1,256]{2,1,0:T(1,128)S(1)}, u32[]{:S(2)}, u32[]{:S(2)}) async-start(f32[64,1,256]{2,1,0:T(1,128)} %shard_map.100), calls=%async_computation | async-start | bytes 131072 | tf_op jit(solution)/shard_map/all_to_all | solution.py:275
  20.8 0.7 copy-start.6
  21.5 36.9 %copy-start.2 = (bf16[2,64,12]{1,0,2:T(2,128)(2,1)S(1)}, bf16[2,64,12]{1,0,2:T(2,128)(2,1)}, u32[]{:S(2)}) copy-start(bf16[2,64,12]{1,0,2:T(2,128)(2,1)} %param.15) | copy-start | bytes 9220
  21.5 36.9 %copy-start.3 = (f32[2,768]{1,0:T(2,128)S(1)}, f32[2,768]{1,0:T(2,128)}, u32[]{:S(2)}) copy-start(f32[2,768]{1,0:T(2,128)} %refs_5_.1) | copy-start | bytes 18436
  21.5 36.9 %copy-start.5 = (s32[64]{0:T(128)S(1)}, s32[64]{0:T(128)}, u32[]{:S(2)}) copy-start(s32[64]{0:T(128)} %param.12) | copy-start | bytes 772
  40.8 36.2 %copy-start.1 = (bf16[2,32,64]{2,1,0:T(8,128)(2,1)S(1)}, bf16[2,32,64]{2,1,0:T(8,128)(2,1)}, u32[]{:S(2)}) copy-start(bf16[2,32,64]{2,1,0:T(8,128)(2,1)} %refs_2_.3) | copy-start | bytes 24580
  40.8 36.2 %copy-start.4 = (f32[2,256]{1,0:T(2,128)S(1)}, f32[2,256]{1,0:T(2,128)}, u32[]{:S(2)}) copy-start(f32[2,256]{1,0:T(2,128)} %refs_3_.3) | copy-start | bytes 6148
  58.4 27.3 %copy-start = (bf16[2,768,1024]{2,1,0:T(8,128)(2,1)S(1)}, bf16[2,768,1024]{2,1,0:T(8,128)(2,1)}, u32[]{:S(2)}) copy-start(bf16[2,768,1024]{2,1,0:T(8,128)(2,1)} %refs_1_.1) | copy-start | bytes 9437188

commit v7 on v6

--- a/solution.py
+++ b/solution.py
@@ -216,7 +216,7 @@
     ).astype(BF16)
 
 
-def next_state(layer, mixed_ref, state_ref, lin_ref, scale_ref):
+def next_state(layer, mixed_ref, state_ref, lin_ref, scale_ref, parts=1):
     rows, width = state_ref.shape
     sources, samples, part = mixed_ref.shape
     made = sources * part // width
@@ -235,36 +235,54 @@
         == (column % samples) * made + column // samples
     )
     mixed = matmul(turn, mixed)
-    joined = []
-    for sample in range(samples):
-        joined.append(mixed[sample * made : (sample + 1) * made])
-        joined.append(
-            matmul(lin_ref[layer], state_ref[sample * tables : (sample + 1) * tables, :])
-        )
-    joined = jnp.concatenate(joined, axis=0) + state_ref[...].astype(F32)
-    return norm_rows(joined, scale_ref[layer : layer + 1, :]).astype(BF16)
+    done = []
+    share = samples // parts
+    for part in range(parts):
+        joined = []
+        for sample in range(part * share, (part + 1) * share):
+            joined.append(mixed[sample * made : (sample + 1) * made])
+            joined.append(
+                matmul(lin_ref[layer], state_ref[sample * tables : (sample + 1) * tables, :])
+            )
+        old = state_ref[part * share * tables : (part + 1) * share * tables, :]
+        joined = jnp.concatenate(joined, axis=0) + old.astype(F32)
+        done.append(norm_rows(joined, scale_ref[layer : layer + 1, :]).astype(BF16))
+    return done
 
 
 def next_layer(
     layer, mixed_ref, old_ref, lin_ref, scale_ref, proj_ref, gain_ref, state_ref, flat_ref
 ):
-    state = next_state(layer, mixed_ref, old_ref, lin_ref, scale_ref)
+    (state,) = next_state(layer, mixed_ref, old_ref, lin_ref, scale_ref)
     state_ref[...] = state
     interactions(state, proj_ref, gain_ref, layer + 1, flat_ref)
 
 
-def last_state(layer, mixed_ref, old_ref, lin_ref, scale_ref, out_ref):
-    out_ref[...] = next_state(layer, mixed_ref, old_ref, lin_ref, scale_ref)
-
-
-def call(kernel, out_shape, *args, own=(), scratch=(), flops=0, limit=SMALL):
+def last_state(layer, mixed_ref, old_ref, lin_ref, scale_ref, out_hbm, part_ref, sems):
+    parts, rows, _ = part_ref.shape
+    copies = []
+    for part, state in enumerate(
+        next_state(layer, mixed_ref, old_ref, lin_ref, scale_ref, parts)
+    ):
+        part_ref[part] = state
+        copies.append(
+            pltpu.make_async_copy(
+                part_ref.at[part], out_hbm.at[pl.ds(part * rows, rows)], sems.at[part]
+            )
+        )
+        copies[-1].start()
+    for copy in copies:
+        copy.wait()
+
+
+def call(kernel, out_shape, *args, own=(), scratch=(), flops=0, limit=SMALL, to=pltpu.VMEM):
     moved = sum(a.size * a.dtype.itemsize for a in (*own, *args))
     return pl.pallas_call(
         kernel,
         out_shape=out_shape,
         in_specs=[pl.BlockSpec(memory_space=pl.ANY)] * len(own)
         + [pl.BlockSpec(memory_space=pltpu.VMEM)] * len(args),
-        out_specs=jax.tree.map(lambda _: pl.BlockSpec(memory_space=pltpu.VMEM), out_shape),
+        out_specs=jax.tree.map(lambda _: pl.BlockSpec(memory_space=to), out_shape),
         scratch_shapes=list(scratch),
         compiler_params=pltpu.CompilerParams(vmem_limit_bytes=limit),
         cost_estimate=pl.CostEstimate(flops=flops, bytes_accessed=moved, transcendentals=0),
@@ -386,6 +404,11 @@
                 state,
                 lin_weight,
                 out_gain,
+                scratch=[
+                    pltpu.VMEM((2, state_rows // 2, width), BF16),
+                    pltpu.SemaphoreType.DMA((2,)),
+                ],
+                to=pl.ANY,
             )
     return state.reshape(samples, tables, width)
 

time: 95.7 us -> 95.7 us (level)
  no operation moved by 1% of the time
where the time goes in v7:
time: 95.7 us; the launch traced here: 95.2 us
  blocking collectives  64.7 us (68%)
  starting transfers between devices  19 us (20%)
  Pallas kernels  9.63 us (10%)
    all_to_all x6, blocking collectives, exchange(): lax.all_to_all(value, axis, 0, 0, tiled=False, axis_index_groups=groups)  64.7 us
    all_to_all x1, starting transfers between devices, exchange(): lax.all_to_all(value, axis, 0, 0, tiled=False, axis_index_groups=groups)  19 us
    pallas_call x9, Pallas kernels, call(): pl.pallas_call(kernel, out_shape=out_shape, in_specs=[pl.BlockSpec(memory...  9.63 us
  transfers between devices with their start and end apart: 1, of which 1 were waited for; matrix products, arithmetic and copies ran while one was open for 0% of the time, Pallas kernels for 3%

profile of v7, /device:TPU:1, one launch (start us, length us, event | category | flops | bytes accessed | tf_op | source)
XLA Modules:
  0.0 95.2 jit_solution(14220848925908410550)
XLA Ops:
  0.0 1.7 %shard_map.100 = f32[64,1,256]{2,1,0:T(1,128)} custom-call(s32[1,64]{1,0:T(1,128)} %bitcast.25, s32[1,64]{1,0:T(1,128)} %bitcast.29, bf16[64,256]{1,0:T(8,128)(2,1)} %bitcast.28), custom_call_target="tpu_custom_call" | custom-call | bytes 33280 | tf_op jit(solution)/shard_map/pallas_call | solution.py:280
  1.7 19.0 %all-to-all-start = ((f32[64,1,256]{2,1,0:T(1,128)}), f32[64,1,256]{2,1,0:T(1,128)S(1)}, u32[]{:S(2)}, u32[]{:S(2)}) async-start(f32[64,1,256]{2,1,0:T(1,128)} %shard_map.100), calls=%async_computation | async-start | bytes 131072 | tf_op jit(solution)/shard_map/all_to_all | solution.py:293
  20.8 0.0 copy-start.6
  20.8 0.7 copy-done.6
  21.5 0.0 copy-start.2
  21.5 0.0 copy-start.3
  21.5 0.0 copy-start.5
  21.5 2.4 %shard_map.101.ordered_ref = bf16[8,64,512]{2,1,0:T(8,128)(2,1)S(1)} custom-call(s32[64,4096]{1,0:T(8,128)} %bitcast.30, s32[32,128]{1,0:T(8,128)S(1)} %bitcast.27), custom_call_target="tpu_custom_call" | custom-call | flops 603979776 | bytes 1064960 | tf_op jit(solution)/shard_map/pallas_call | solution.py:280
  23.9 0.9 all-to-all-done.arrived_ref
  24.8 0.2 shard_map.102
  25.1 15.4 %all_to_all.35 = bf16[8,64,768]{2,1,0:T(8,128)(2,1)S(1)} all-to-all(bf16[8,64,768]{2,1,0:T(8,128)(2,1)S(1)} %shard_map.102), channel_id=1, replica_groups={{5,6,7,0,1,2,3,4},{13,14,15,8,9,10,11,12},{21,22,23,16,17,18,19,20},{29..., dimensions={0} | all-to-all | bytes 1572864 | tf_op jit(solution)/shard_map/all_to_all | solution.py:293
  40.4 0.3 shard_map.103
  40.8 0.0 copy-start.1
  40.8 0.0 copy-start.4
  40.8 17.6 %all_to_all.36 = bf16[64,8,256]{2,1,0:T(8,128)(2,1)S(1)} all-to-all(bf16[64,8,256]{2,1,0:T(8,128)(2,1)S(1)} %bitcast.18), channel_id=1, replica_groups={{288,296,304,312,256,264,272,280,352,360,368,376,320,328,336,344,416,42..., dimensions={0} | all-to-all | bytes 524288 | tf_op jit(solution)/shard_map/all_to_all | solution.py:293
  58.4 0.0 copy-done.2
  58.4 0.0 copy-done.3
  58.4 0.0 copy-done.5
  58.4 0.0 copy-start
  58.4 1.6 %shard_map.104 = (bf16[512,256]{1,0:T(8,128)(2,1)S(1)}, bf16[8,8,768]{2,1,0:T(8,128)(2,1)S(1)}, bf16[1,768,1024]{2,1,0:T(8,128)(2,1)S(1)}) custom-call(bf16[2,768,1024]{2,1,0:T(8,128)(2,1)} %refs_1_.1, bf16[512,256]{1,0:T(8,128)(2,1)S(1)} %bitcast.17, s32[1,64]{1,0:T(1,128)S(1)} %bitcast.26, bf16[12,2,64]{2,1,0:T(2,128)(2,1)S(1)} %bitcast.23, ...), custom_call_target="tpu_custom_call" | custom-call | bytes 3417344 | tf_op jit(solution)/shard_map/pallas_call | solution.py:280
  60.0 8.9 %all_to_all.37 = bf16[8,8,768]{2,1,0:T(8,128)(2,1)S(1)} all-to-all(bf16[8,8,768]{2,1,0:T(8,128)(2,1)S(1)} %get-tuple-element.10), channel_id=1, replica_groups={{5,6,7,0,1,2,3,4},{13,14,15,8,9,10,11,12},{21,22,23,16,17,18,19,20},{29..., dimensions={0} | all-to-all | bytes 196608 | tf_op jit(solution)/shard_map/all_to_all | solution.py:293
  68.9 0.6 shard_map.105
  69.6 7.4 %all_to_all.38.refs_0_ = bf16[8,8,1024]{2,1,0:T(8,128)(2,1)S(1)} all-to-all(bf16[8,8,1024]{2,1,0:T(8,128)(2,1)S(1)} %bitcast.19), channel_id=1, replica_groups={{5,6,7,0,1,2,3,4},{13,14,15,8,9,10,11,12},{21,22,23,16,17,18,19,20},{29..., dimensions={0} | all-to-all | bytes 262144 | tf_op jit(solution)/shard_map/all_to_all | solution.py:293
  77.0 0.0 copy-done.1
  77.0 0.0 copy-done.4
  77.0 1.0 %shard_map.106 = (bf16[512,256]{1,0:T(8,128)(2,1)S(1)}, bf16[8,8,768]{2,1,0:T(8,128)(2,1)S(1)}) custom-call(bf16[8,8,1024]{2,1,0:T(8,128)(2,1)S(1)} %all_to_all.38.refs_0_, bf16[512,256]{1,0:T(8,128)(2,1)S(1)} %get-tuple-element.12.refs_1_, bf16[2,32,64]{2,1,0:T(8,128)(2,1)S(1)} %copy-done.1, f32[2,256]{1,0:T(2,128)S(1)} %copy-done.4, ...), custom_call_target="tpu_custom_call" | custom-call | bytes 412672 | tf_op jit(solution)/shard_map/pallas_call | solution.py:280
  78.0 7.7 %all_to_all.39 = bf16[8,8,768]{2,1,0:T(8,128)(2,1)S(1)} all-to-all(bf16[8,8,768]{2,1,0:T(8,128)(2,1)S(1)} %get-tuple-element.13), channel_id=1, replica_groups={{5,6,7,0,1,2,3,4},{13,14,15,8,9,10,11,12},{21,22,23,16,17,18,19,20},{29..., dimensions={0} | all-to-all | bytes 196608 | tf_op jit(solution)/shard_map/all_to_all | solution.py:293
  85.7 0.0 copy-done
  85.7 0.6 shard_map.107
  86.4 7.7 %all_to_all.40.refs_0_ = bf16[8,8,1024]{2,1,0:T(8,128)(2,1)S(1)} all-to-all(bf16[8,8,1024]{2,1,0:T(8,128)(2,1)S(1)} %bitcast.20), channel_id=1, replica_groups={{5,6,7,0,1,2,3,4},{13,14,15,8,9,10,11,12},{21,22,23,16,17,18,19,20},{29..., dimensions={0} | all-to-all | bytes 262144 | tf_op jit(solution)/shard_map/all_to_all | solution.py:293
  94.1 1.1 %shard_map.108 = bf16[512,256]{1,0:T(8,128)(2,1)} custom-call(bf16[8,8,1024]{2,1,0:T(8,128)(2,1)S(1)} %all_to_all.40.refs_0_, bf16[512,256]{1,0:T(8,128)(2,1)S(1)} %get-tuple-element.14.refs_1_, bf16[2,32,64]{2,1,0:T(8,128)(2,1)S(1)} %copy-done.1, f32[2,256]{1,0:T(2,128)S(1)} %copy-done.4), custom_call_target="tpu_custom_call" | custom-call | bytes 403456 | tf_op jit(solution)/shard_map/pallas_call | solution.py:280
Async XLA Ops:
  1.7 23.1 %all-to-all-start = ((f32[64,1,256]{2,1,0:T(1,128)}), f32[64,1,256]{2,1,0:T(1,128)S(1)}, u32[]{:S(2)}, u32[]{:S(2)}) async-start(f32[64,1,256]{2,1,0:T(1,128)} %shard_map.100), calls=%async_computation | async-start | bytes 131072 | tf_op jit(solution)/shard_map/all_to_all | solution.py:293
  20.8 0.7 copy-start.6
  21.5 36.9 %copy-start.2 = (bf16[2,64,12]{1,0,2:T(2,128)(2,1)S(1)}, bf16[2,64,12]{1,0,2:T(2,128)(2,1)}, u32[]{:S(2)}) copy-start(bf16[2,64,12]{1,0,2:T(2,128)(2,1)} %param.15) | copy-start | bytes 9220
  21.5 36.9 %copy-start.3 = (f32[2,768]{1,0:T(2,128)S(1)}, f32[2,768]{1,0:T(2,128)}, u32[]{:S(2)}) copy-start(f32[2,768]{1,0:T(2,128)} %refs_5_.1) | copy-start | bytes 18436
  21.5 36.9 %copy-start.5 = (s32[64]{0:T(128)S(1)}, s32[64]{0:T(128)}, u32[]{:S(2)}) copy-start(s32[64]{0:T(128)} %param.12) | copy-start | bytes 772
  40.8 36.2 %copy-start.1 = (bf16[2,32,64]{2,1,0:T(8,128)(2,1)S(1)}, bf16[2,32,64]{2,1,0:T(8,128)(2,1)}, u32[]{:S(2)}) copy-start(bf16[2,32,64]{2,1,0:T(8,128)(2,1)} %refs_2_.3) | copy-start | bytes 24580
  40.8 36.2 %copy-start.4 = (f32[2,256]{1,0:T(2,128)S(1)}, f32[2,256]{1,0:T(2,128)}, u32[]{:S(2)}) copy-start(f32[2,256]{1,0:T(2,128)} %refs_3_.3) | copy-start | bytes 6148
  58.4 27.3 %copy-start = (bf16[2,768,1024]{2,1,0:T(8,128)(2,1)S(1)}, bf16[2,768,1024]{2,1,0:T(8,128)(2,1)}, u32[]{:S(2)}) copy-start(bf16[2,768,1024]{2,1,0:T(8,128)(2,1)} %refs_1_.1) | copy-start | bytes 9437188
